TPU v7x, 128 devices: a whole 4x4x4 slice. The times are simulated.
128 devices in a mesh: grp: 4 (over z_hi, core), seq: 32 (over z_lo, y, x).
Axes of the slice: x: 4, y: 4, z: 4 (z_hi: 2, z_lo: 2; z = z_hi * 2 + z_lo), core: 2. Of those that a mesh axis runs over, the one named last changes fastest.
Arguments:
- query: bfloat16 [4, 4096, 4096], P('grp', 'seq'), may hold values from -10 to 10
- key: bfloat16 [4, 4096, 4096], P('grp', 'seq'), may hold values from -10 to 10
- value: bfloat16 [4, 4096, 4096], P('grp', 'seq'), may hold values from -24 to 24
- gain_query: float32 [4096], replicated, may hold values from 0.1 to 1.9
- gain_key: float32 [4096], replicated, may hold values from 0.1 to 1.9
- ctrl_query: bfloat16 [4, 1024, 4096], P('grp', 'seq'), may hold values from -10 to 10
- ctrl_key: bfloat16 [4, 1024, 4096], P('grp', 'seq'), may hold values from -10 to 10
- ctrl_value: bfloat16 [4, 1024, 4096], P('grp', 'seq'), may hold values from -24 to 24
- ctrl_gain_query: float32 [4096], replicated, may hold values from 0.1 to 1.9
- ctrl_gain_key: float32 [4096], replicated, may hold values from 0.1 to 1.9
- gate_table: float32 [16, 4096], replicated, may hold values from 2 to 16
- levels: int32 [4, 8], P('grp'), may hold values from 0 to 15
- frame_map: int32 [4, 4096], P('grp', 'seq'), may hold values from 0 to 7, never falling along the last dimension, each value on 1 to 1024 neighbouring positions
- control_match: int32 [4, 1024], P('grp', 'seq'), may hold values from 0 to 4095, as said below
Outputs:
- mixed: bfloat16 [4, 4096, 4096], P('grp', 'seq')
Inputs may be any that keep to these rules, and one draw needn't show every extreme that they name: `control_match`: the 1024 entries of one video are distinct.
All inputs are finite; a program needn't handle non-finite values.
Results may differ from a plain program's by a relative error of at most 0.0055.
The roundings to bfloat16 on the way count: a program that leaves them out, or rounds other values in their place, can miss the bound.
Values may be sent and summed in bfloat16 or wider, within the bound.
No kernel may reach another device: no remote copies, remote signals or barrier semaphores. Data moves between devices by JAX's collectives and lax.ppermute only.
A program may use at most 64 MiB of HBM per device.

v0:
```python
import math

import jax
import jax.numpy as jnp
from jax import lax
from jax.sharding import PartitionSpec as P

HEADS = 32
HEAD_DIM = 128
WIDTH = 4096
TOK_DEV = 128
CTRL_DEV = 32
FRAMES = 8
LEVELS = 16


def from_behind(block, axis, distance):
    devices = range(lax.axis_size(axis))
    route = [((i - distance) % len(devices), i) for i in devices]
    return lax.ppermute(block, axis, route)


def rms_round(values, gain):
    wide = values.astype(jnp.float32)
    mean_sq = jnp.mean(wide * wide, axis=-1, keepdims=True)
    return (wide * lax.rsqrt(mean_sq + 1e-06) * gain).astype(jnp.bfloat16)


def attend_head(queries, keys, values, query_frames, key_frames, causal):
    rows = queries.shape[0]
    block = min(512, rows)
    factor = 1.0 / math.sqrt(keys.shape[1])
    q_blocks = queries.reshape(rows // block, block, queries.shape[1])
    if causal:
        f_blocks = query_frames.reshape(rows // block, block)
    else:
        f_blocks = jnp.zeros((rows // block, block), jnp.int32)

    def one_block(pair):
        part, frames = pair
        scores = jnp.dot(part, keys.T, preferred_element_type=jnp.float32) * factor
        if causal:
            scores = jnp.where(key_frames[None, :] <= frames[:, None], scores, -1e30)
        top = jnp.max(scores, axis=1, keepdims=True)
        expo = jnp.exp(scores - top)
        weights = (expo / jnp.sum(expo, axis=1, keepdims=True)).astype(jnp.bfloat16)
        return jnp.dot(weights, values, preferred_element_type=jnp.float32).astype(jnp.bfloat16)

    result = lax.map(one_block, (q_blocks, f_blocks))
    return result.reshape(rows, values.shape[1])


def attend_items(pieces, query_frames, key_frames, causal):
    q_first = jnp.moveaxis(pieces[0][:, 0], 1, 0)
    k_first = jnp.moveaxis(pieces[1][:, 0], 1, 0)
    v_first = jnp.moveaxis(pieces[2][:, 0], 1, 0)

    def one_head(triple):
        return attend_head(triple[0], triple[1], triple[2], query_frames, key_frames, causal)

    result = lax.map(one_head, (q_first, k_first, v_first))
    return jnp.moveaxis(result, 0, 1)[:, None]


def gate_rows(frames, frame_levels, table):
    picks = frames[:, None] == jnp.arange(FRAMES, dtype=jnp.int32)[None, :]
    row_levels = jnp.sum(jnp.where(picks, frame_levels[None, :], 0), axis=1)
    onehot = (row_levels[:, None] == jnp.arange(LEVELS, dtype=jnp.int32)[None, :]).astype(
        jnp.float32
    )
    return jnp.dot(onehot, table, precision=lax.Precision.HIGHEST)


def body(
    query,
    key,
    value,
    gain_query,
    gain_key,
    ctrl_query,
    ctrl_key,
    ctrl_value,
    ctrl_gain_query,
    ctrl_gain_key,
    gate_table,
    levels,
    frame_map,
    control_match,
):
    parts = lax.axis_size("seq")
    local_heads = HEADS // parts
    main_shape = (TOK_DEV, parts, local_heads, HEAD_DIM)
    ctrl_shape = (CTRL_DEV, parts, local_heads, HEAD_DIM)
    q_main = rms_round(query[0], gain_query).reshape(main_shape)
    k_main = rms_round(key[0], gain_key).reshape(main_shape)
    v_main = value[0].reshape(main_shape)
    q_ctrl = rms_round(ctrl_query[0], ctrl_gain_query).reshape(ctrl_shape)
    k_ctrl = rms_round(ctrl_key[0], ctrl_gain_key).reshape(ctrl_shape)
    v_ctrl = ctrl_value[0].reshape(ctrl_shape)
    frames_local = frame_map[0]
    frame_levels = levels[0]
    frames_all = lax.all_gather(frames_local, "seq", axis=0, tiled=True)
    attn = attend_items(
        (
            lax.all_to_all(q_main, "seq", split_axis=1, concat_axis=0, tiled=True),
            lax.all_to_all(k_main, "seq", split_axis=1, concat_axis=0, tiled=True),
            lax.all_to_all(v_main, "seq", split_axis=1, concat_axis=0, tiled=True),
        ),
        frames_all,
        frames_all,
        True,
    )
    ctrl_attn = attend_items(
        (
            lax.all_to_all(q_ctrl, "seq", split_axis=1, concat_axis=0, tiled=True),
            lax.all_to_all(k_ctrl, "seq", split_axis=1, concat_axis=0, tiled=True),
            lax.all_to_all(v_ctrl, "seq", split_axis=1, concat_axis=0, tiled=True),
        ),
        None,
        None,
        False,
    )
    attn_rows = lax.all_to_all(attn, "seq", split_axis=0, concat_axis=1, tiled=True).reshape(
        TOK_DEV, WIDTH
    )
    ctrl_rows = lax.all_to_all(ctrl_attn, "seq", split_axis=0, concat_axis=1, tiled=True).reshape(
        CTRL_DEV, WIDTH
    )
    hint_rows = from_behind(ctrl_rows, "grp", 1)
    my_start = lax.axis_index("seq") * TOK_DEV
    empty = jnp.zeros((TOK_DEV, WIDTH), jnp.float32)
    rows_in = lax.all_gather(hint_rows, "seq", axis=0, tiled=True)
    matches = lax.all_gather(control_match[0], "seq", axis=0, tiled=True)
    local = matches - my_start
    valid = (local >= 0) & (local < TOK_DEV)
    target = jnp.where(valid, local, TOK_DEV).astype(jnp.int32)
    added = empty.at[target].add(rows_in.astype(jnp.float32), mode="drop")
    gate = gate_rows(frames_local, frame_levels, gate_table)
    mixed = (gate * attn_rows.astype(jnp.float32) + added).astype(jnp.bfloat16)
    return mixed[None]


def solution(mesh):
    return jax.shard_map(
        body,
        mesh=mesh,
        in_specs=(
            P("grp", "seq", None),
            P("grp", "seq", None),
            P("grp", "seq", None),
            P(),
            P(),
            P("grp", "seq", None),
            P("grp", "seq", None),
            P("grp", "seq", None),
            P(),
            P(),
            P(),
            P("grp", None),
            P("grp", "seq"),
            P("grp", "seq"),
        ),
        out_specs=P("grp", "seq", None),
        check_vma=False,
    )
```

profile of v0, /device:TPU:64, one launch (start us, length us, event | category | flops | bytes accessed | tf_op | source)
XLA Modules:
  0.0 398.9 jit_solution(12073535421069820681)
XLA Ops:
  6.5 1.0 convert_bitcast_fusion.3
  7.6 1.1 fusion.18
  9.0 0.8 copy.55
  9.8 8.4 %all-to-all-start.4 = ((bf16[32,32,1,128]{3,0,2,1:T(8,128)(2,1)}), bf16[32,32,1,128]{3,0,2,1:T(8,128)(2,1)S(1)}, u32[]{:S(2)}, u32[]{:S(2)}) async-start(bf16[32,32,1,128]{3,0,2,1:T(8,128)(2,1)} %copy.55), calls=%async_computation.4 | async-start | bytes 524288 | tf_op jit(solution)/shard_map/all_to_all | solution.py:115
  18.7 0.8 copy.56
  19.5 7.7 %all-to-all-done.4 = bf16[32,32,1,128]{3,0,2,1:T(8,128)(2,1)S(1)} async-done(((bf16[32,32,1,128]{3,0,2,1:T(8,128)(2,1)}), bf16[32,32,1,128]{3,0,2,1:T(8,128)(2,1)S(1)}, u32[]{:S(2)}, u32[]{:S(2)}) %all-to-all-start.4) | async-done | bytes 262176 | tf_op jit(solution)/shard_map/all_to_all | solution.py:115
  27.1 4.0 %all-to-all-start.5 = ((bf16[32,32,1,128]{3,0,2,1:T(8,128)(2,1)}), bf16[32,32,1,128]{3,0,2,1:T(8,128)(2,1)S(1)}, u32[]{:S(2)}, u32[]{:S(2)}) async-start(bf16[32,32,1,128]{3,0,2,1:T(8,128)(2,1)} %copy.56), calls=%async_computation.5 | async-start | bytes 524288 | tf_op jit(solution)/shard_map/all_to_all | solution.py:116
  31.2 0.7 copy.46
  31.9 0.8 copy.57
  32.7 7.4 %all-to-all-done.5 = bf16[32,32,1,128]{3,0,2,1:T(8,128)(2,1)S(1)} async-done(((bf16[32,32,1,128]{3,0,2,1:T(8,128)(2,1)}), bf16[32,32,1,128]{3,0,2,1:T(8,128)(2,1)S(1)}, u32[]{:S(2)}, u32[]{:S(2)}) %all-to-all-start.5) | async-done | bytes 262176 | tf_op jit(solution)/shard_map/all_to_all | solution.py:116
  40.1 4.1 %all-to-all-start.6 = ((bf16[32,32,1,128]{3,0,2,1:T(8,128)(2,1)}), bf16[32,32,1,128]{3,0,2,1:T(8,128)(2,1)S(1)}, u32[]{:S(2)}, u32[]{:S(2)}) async-start(bf16[32,32,1,128]{3,0,2,1:T(8,128)(2,1)} %copy.57), calls=%async_computation.6 | async-start | bytes 524288 | tf_op jit(solution)/shard_map/all_to_all | solution.py:117
  44.8 8.4 %all-to-all-done.6 = bf16[32,32,1,128]{3,0,2,1:T(8,128)(2,1)S(1)} async-done(((bf16[32,32,1,128]{3,0,2,1:T(8,128)(2,1)}), bf16[32,32,1,128]{3,0,2,1:T(8,128)(2,1)S(1)}, u32[]{:S(2)}, u32[]{:S(2)}) %all-to-all-start.6) | async-done | bytes 262176 | tf_op jit(solution)/shard_map/all_to_all | solution.py:117
  53.1 3.4 while.35
  57.2 0.8 reduce.9
  57.9 0.8 reshape.278
  58.7 4.1 %all-to-all-start.7 = ((bf16[32,2,2048]{2,1,0:T(2,128)(2,1)}), bf16[32,2,2048]{2,1,0:T(2,128)(2,1)S(1)}, u32[]{:S(2)}, u32[]{:S(2)}) async-start(bf16[32,2,2048]{2,1,0:T(2,128)(2,1)} %reshape.278), calls=%async_computation.7 | async-start | bytes 524288 | tf_op jit(solution)/shard_map/all_to_all | solution.py:126
  62.8 0.7 multiply_convert_fusion.1
  63.5 1.3 copy.47
  64.8 6.9 %all-to-all-done.7 = bf16[32,2,2048]{2,1,0:T(2,128)(2,1)S(1)} async-done(((bf16[32,2,2048]{2,1,0:T(2,128)(2,1)}), bf16[32,2,2048]{2,1,0:T(2,128)(2,1)S(1)}, u32[]{:S(2)}, u32[]{:S(2)}) %all-to-all-start.7) | async-done | bytes 262176 | tf_op jit(solution)/shard_map/all_to_all | solution.py:126
  71.7 4.7 %all-to-all-start = ((bf16[128,32,1,128]{3,0,2,1:T(8,128)(2,1)}), bf16[128,32,1,128]{3,0,2,1:T(8,128)(2,1)}, u32[]{:S(2)}, u32[]{:S(2)}) async-start(bf16[128,32,1,128]{3,0,2,1:T(8,128)(2,1)} %copy.47), calls=%async_computation | async-start | bytes 2097152 | tf_op jit(solution)/shard_map/all_to_all | solution.py:105
  77.6 0.7 multiply_convert_fusion
  78.4 1.3 copy.49
  79.7 9.3 %all-to-all-done = bf16[128,32,1,128]{3,0,2,1:T(8,128)(2,1)} async-done(((bf16[128,32,1,128]{3,0,2,1:T(8,128)(2,1)}), bf16[128,32,1,128]{3,0,2,1:T(8,128)(2,1)}, u32[]{:S(2)}, u32[]{:S(2)}) %all-to-all-start) | async-done | bytes 1048608 | tf_op jit(solution)/shard_map/all_to_all | solution.py:105
  89.0 4.7 %all-to-all-start.1 = ((bf16[128,32,1,128]{3,0,2,1:T(8,128)(2,1)}), bf16[128,32,1,128]{3,0,2,1:T(8,128)(2,1)}, u32[]{:S(2)}, u32[]{:S(2)}) async-start(bf16[128,32,1,128]{3,0,2,1:T(8,128)(2,1)} %copy.49), calls=%async_computation.1 | async-start | bytes 2097152 | tf_op jit(solution)/shard_map/all_to_all | solution.py:106
  94.3 1.3 copy.51
  95.6 10.6 %all-to-all-done.1 = bf16[128,32,1,128]{3,0,2,1:T(8,128)(2,1)} async-done(((bf16[128,32,1,128]{3,0,2,1:T(8,128)(2,1)}), bf16[128,32,1,128]{3,0,2,1:T(8,128)(2,1)}, u32[]{:S(2)}, u32[]{:S(2)}) %all-to-all-start.1) | async-done | bytes 1048608 | tf_op jit(solution)/shard_map/all_to_all | solution.py:106
  106.2 4.7 %all-to-all-start.2 = ((bf16[128,32,1,128]{3,0,2,1:T(8,128)(2,1)}), bf16[128,32,1,128]{3,0,2,1:T(8,128)(2,1)}, u32[]{:S(2)}, u32[]{:S(2)}) async-start(bf16[128,32,1,128]{3,0,2,1:T(8,128)(2,1)} %copy.51), calls=%async_computation.2 | async-start | bytes 2097152 | tf_op jit(solution)/shard_map/all_to_all | solution.py:107
  111.6 81.1 %all-gather = s32[1,4096]{1,0:T(1,128)S(1)} all-gather(s32[1,128]{1,0:T(1,128)S(1)} %copy-done.11), channel_id=2, replica_groups=mesh['grp'=4,'seq'=32] {'seq'}, dimensions={1}, use_global_device_ids=true | all-gather | bytes 16896 | tf_op jit(solution)/shard_map/all_gather | solution.py:102
  193.9 0.7 copy-done.6
  194.6 56.7 %while.34 = (s32[]{:T(128)}, bf16[8,512,128]{2,1,0:T(8,128)(2,1)S(1)}, s32[4096]{0:T(1024)S(1)}, s32[8,512]{1,0:T(8,128)S(1)}, bf16[8,512,128]{2,1,0:T(8,128)(2,...) while((s32[]{:T(128)}, bf16[8,512,128]{2,1,0:T(8,128)(2,1)S(1)}, ...), condition=%wide.region_6.7_spmd, body=%wide.region_3.6_spmd.sunk | while | flops 1092680704 | bytes 27558492 | solution.py:49
  194.6 2.9 fusion.42
  197.6 1.3 fusion.43
  198.9 2.8 fusion.44
  201.7 2.9 fusion.42
  204.7 1.3 fusion.43
  205.9 2.8 fusion.44
  208.8 3.0 fusion.42
  211.7 1.3 fusion.43
  213.0 2.8 fusion.44
  215.9 3.0 fusion.42
  218.8 1.3 fusion.43
  220.1 2.8 fusion.44
  223.0 3.0 fusion.42
  225.9 1.3 fusion.43
  227.2 2.8 fusion.44
  230.1 3.0 fusion.42
  233.0 1.3 fusion.43
  234.3 2.8 fusion.44
  237.1 3.0 fusion.42
  240.1 1.3 fusion.43
  241.4 2.8 fusion.44
  244.2 3.0 fusion.42
  247.2 1.3 fusion.43
  248.5 2.8 fusion.44
  251.3 1.4 reduce.8
  252.8 1.1 reshape.276
  253.9 3.9 all-to-all-start.3
  259.1 27.0 %all-reduce = s32[1024]{0:T(1024)S(1)} all-reduce(s32[1024]{0:T(1024)S(1)} %bitcast_dynamic-update-slice_fusion), channel_id=3, replica_groups=mesh['grp'=4,'seq'=32] {'seq'}, use_global_device_ids=true, to_apply=%add | all-reduce | flops 1024 | bytes 8192
  286.2 1.1 reshape.277
  287.7 1.2 copy.54
  288.9 2.1 convolution_multiply_fusion
  291.1 74.5 %all-gather.4.cloned.1.call-done = bf16[1024,4096]{1,0:T(8,128)(2,1)} async-done(((bf16[32,4096]{1,0:T(8,128)(2,1)}), bf16[1024,4096]{1,0:T(8,128)(2,1)}) %all-gather.4.cloned.1.call-update) | async-done | bytes 8388624 | tf_op jit(solution)/shard_map/all_gather | solution.py:132
  365.6 25.4 %scatter_custom_fusion = f32[128,4096]{1,0:T(8,128)S(1)} fusion(f32[128,4096]{1,0:T(8,128)S(1)} %convolution_multiply_fusion, s32[1024]{0:T(1024)S(1)} %compare_select_fusion, bf16[1024,4096]{1,0:T(8,128)(2,1)} %all-gather.4.cloned.1.call-done), kind=kCustom, calls=%fused_computation.25 | custom fusion | flops 8388608 | bytes 10485760 | tf_op jit(solution)/shard_map/scatter-add | solution.py:137
  390.9 1.1 convert_bitcast_fusion.1
  (81 shorter events, 10.3 us)
Async XLA Ops:
  6.5 282.4 %copy-start = (f32[16,4096]{1,0:T(8,128)S(1)}, f32[16,4096]{1,0:T(8,128)}, u32[]{:S(2)}) copy-start(f32[16,4096]{1,0:T(8,128)} %param.28) | copy-start | bytes 786436
  6.5 2.3 copy-start.9
  6.5 11.6 %copy-start.1 = (bf16[1,32,4096]{2,1,0:T(8,128)(2,1)S(1)}, bf16[1,32,4096]{2,1,0:T(8,128)(2,1)}, u32[]{:S(2)}) copy-start(bf16[1,32,4096]{2,1,0:T(8,128)(2,1)} %param.24) | copy-start | bytes 786436
  8.8 9.7 %copy-start.10 = (f32[4096]{0:T(1024)S(1)}, f32[4096]{0:T(1024)}, u32[]{:S(2)}) copy-start(f32[4096]{0:T(1024)} %param.27) | copy-start | bytes 49156
  9.8 17.4 %all-to-all-start.4 = ((bf16[32,32,1,128]{3,0,2,1:T(8,128)(2,1)}), bf16[32,32,1,128]{3,0,2,1:T(8,128)(2,1)S(1)}, u32[]{:S(2)}, u32[]{:S(2)}) async-start(bf16[32,32,1,128]{3,0,2,1:T(8,128)(2,1)} %copy.55), calls=%async_computation.4 | async-start | bytes 524288 | tf_op jit(solution)/shard_map/all_to_all | solution.py:115
  18.2 13.0 %copy-start.2 = (bf16[1,128,4096]{2,1,0:T(8,128)(2,1)S(1)}, bf16[1,128,4096]{2,1,0:T(8,128)(2,1)}, u32[]{:S(2)}) copy-start(bf16[1,128,4096]{2,1,0:T(8,128)(2,1)} %param.18) | copy-start | bytes 3145732
  18.5 13.4 %copy-start.5 = (bf16[1,32,4096]{2,1,0:T(8,128)(2,1)S(1)}, bf16[1,32,4096]{2,1,0:T(8,128)(2,1)}, u32[]{:S(2)}) copy-start(bf16[1,32,4096]{2,1,0:T(8,128)(2,1)} %param.25) | copy-start | bytes 786436
  27.1 13.0 %all-to-all-start.5 = ((bf16[32,32,1,128]{3,0,2,1:T(8,128)(2,1)}), bf16[32,32,1,128]{3,0,2,1:T(8,128)(2,1)S(1)}, u32[]{:S(2)}, u32[]{:S(2)}) async-start(bf16[32,32,1,128]{3,0,2,1:T(8,128)(2,1)} %copy.56), calls=%async_computation.5 | async-start | bytes 524288 | tf_op jit(solution)/shard_map/all_to_all | solution.py:116
  40.1 13.0 %all-to-all-start.6 = ((bf16[32,32,1,128]{3,0,2,1:T(8,128)(2,1)}), bf16[32,32,1,128]{3,0,2,1:T(8,128)(2,1)S(1)}, u32[]{:S(2)}, u32[]{:S(2)}) async-start(bf16[32,32,1,128]{3,0,2,1:T(8,128)(2,1)} %copy.57), calls=%async_computation.6 | async-start | bytes 524288 | tf_op jit(solution)/shard_map/all_to_all | solution.py:117
  53.1 9.7 %copy-start.7 = (f32[4096]{0:T(1024)S(1)}, f32[4096]{0:T(1024)}, u32[]{:S(2)}) copy-start(f32[4096]{0:T(1024)} %param.21) | copy-start | bytes 49156
  58.7 13.0 %all-to-all-start.7 = ((bf16[32,2,2048]{2,1,0:T(2,128)(2,1)}), bf16[32,2,2048]{2,1,0:T(2,128)(2,1)S(1)}, u32[]{:S(2)}, u32[]{:S(2)}) async-start(bf16[32,2,2048]{2,1,0:T(2,128)(2,1)} %reshape.278), calls=%async_computation.7 | async-start | bytes 524288 | tf_op jit(solution)/shard_map/all_to_all | solution.py:126
  64.8 11.6 %copy-start.3 = (bf16[1,128,4096]{2,1,0:T(8,128)(2,1)S(1)}, bf16[1,128,4096]{2,1,0:T(8,128)(2,1)}, u32[]{:S(2)}) copy-start(bf16[1,128,4096]{2,1,0:T(8,128)(2,1)} %param.19) | copy-start | bytes 3145732
  71.7 17.3 %all-to-all-start = ((bf16[128,32,1,128]{3,0,2,1:T(8,128)(2,1)}), bf16[128,32,1,128]{3,0,2,1:T(8,128)(2,1)}, u32[]{:S(2)}, u32[]{:S(2)}) async-start(bf16[128,32,1,128]{3,0,2,1:T(8,128)(2,1)} %copy.47), calls=%async_computation | async-start | bytes 2097152 | tf_op jit(solution)/shard_map/all_to_all | solution.py:105
  76.4 1.2 copy-start.8
  79.7 14.0 %copy-start.4 = (bf16[1,128,4096]{2,1,0:T(8,128)(2,1)S(1)}, bf16[1,128,4096]{2,1,0:T(8,128)(2,1)}, u32[]{:S(2)}) copy-start(bf16[1,128,4096]{2,1,0:T(8,128)(2,1)} %param.20) | copy-start | bytes 3145732
  89.0 17.3 %all-to-all-start.1 = ((bf16[128,32,1,128]{3,0,2,1:T(8,128)(2,1)}), bf16[128,32,1,128]{3,0,2,1:T(8,128)(2,1)}, u32[]{:S(2)}, u32[]{:S(2)}) async-start(bf16[128,32,1,128]{3,0,2,1:T(8,128)(2,1)} %copy.49), calls=%async_computation.1 | async-start | bytes 2097152 | tf_op jit(solution)/shard_map/all_to_all | solution.py:106
  95.6 16.0 %copy-start.11 = (s32[1,128]{1,0:T(1,128)S(1)}, s32[1,128]{1,0:T(1,128)}, u32[]{:S(2)}) copy-start(s32[1,128]{1,0:T(1,128)} %param.30) | copy-start | bytes 1540
  106.2 88.4 %all-to-all-start.2 = ((bf16[128,32,1,128]{3,0,2,1:T(8,128)(2,1)}), bf16[128,32,1,128]{3,0,2,1:T(8,128)(2,1)}, u32[]{:S(2)}, u32[]{:S(2)}) async-start(bf16[128,32,1,128]{3,0,2,1:T(8,128)(2,1)} %copy.51), calls=%async_computation.2 | async-start | bytes 2097152 | tf_op jit(solution)/shard_map/all_to_all | solution.py:107
  110.9 254.7 %all-gather.4.cloned.1.call-start = ((), (), s32[]{:S(2)}) async-start(), calls=%async_computation.8 | async-start | bytes 8650752 | tf_op jit(solution)/shard_map/all_gather | solution.py:132
  111.5 82.4 %collective-permute-start = (bf16[32,4096]{1,0:T(8,128)(2,1)S(1)}, bf16[32,4096]{1,0:T(8,128)(2,1)S(1)}, u32[]{:S(2)}, u32[]{:S(2)}) collective-permute-start(bf16[32,4096]{1,0:T(8,128)(2,1)S(1)} %bitcast.150), channel_id=1, source_target_pairs={{96,0},{0,32},{32,64},{64,96},{97,1},{1,33},{33,65},{65,97},{98,2}... | collective-permute-start | bytes 786440 | tf_op jit(solution)/shard_map/ppermute | solution.py:20
  193.9 0.7 copy-start.6
  252.7 5.1 %copy-start.14 = (u32[128]{0:T(128)S(1)}, u32[128]{0:T(128)}, u32[]{:S(2)}) copy-start(u32[128]{0:T(128)} %constant.97) | copy-start | bytes 1540
  252.8 6.2 %copy-start.12 = (s32[1,32]{1,0:T(1,128)S(1)}, s32[1,32]{1,0:T(1,128)}, u32[]{:S(2)}) copy-start(s32[1,32]{1,0:T(1,128)} %param.31) | copy-start | bytes 388
  252.8 33.4 %copy-start.13 = (s32[1,8]{1,0:T(1,128)S(1)}, s32[1,8]{1,0:T(1,128)}, u32[]{:S(2)}) copy-start(s32[1,8]{1,0:T(1,128)} %param.29) | copy-start | bytes 100
  253.9 32.4 %all-to-all-start.3 = ((bf16[32,2,8192]{2,1,0:T(2,128)(2,1)}), bf16[32,2,8192]{2,1,0:T(2,128)(2,1)S(1)}, u32[]{:S(2)}, u32[]{:S(2)}) async-start(bf16[32,2,8192]{2,1,0:T(2,128)(2,1)} %reshape.276), calls=%async_computation.3 | async-start | bytes 2097152 | tf_op jit(solution)/shard_map/all_to_all | solution.py:123
Sparse Core Ops, SparseCore 0:
  194.7 170.7 all-gather.3
where the time goes:
time: 400 us; the launch traced here: 399 us
  waiting for transfers between devices  125 us (31%)
  blocking collectives  108 us (27%)
  matrix products  50.7 us (13%)
  other arithmetic  46.1 us (12%)
  starting transfers between devices  38.6 us (10%)
  local copies, waits for them, and re-layouts  16 us (4%)
  between operations  14.5 us (4%)
    all_gather x1, blocking collectives, body(): frames_all = lax.all_gather(frames_local, 'seq', axis=0, tiled=True)  81.1 us
    all_gather x1, waiting for transfers between devices, body(): rows_in = lax.all_gather(hint_rows, 'seq', axis=0, tiled=True)  74.5 us
    unnamed x1, blocking collectives  27 us
    scatter-add x1, other arithmetic, body(): added = empty.at[target].add(rows_in.astype(jnp.float32), mode='drop')  25.4 us
    dot_general x10, matrix products, one_block(): scores = jnp.dot(part, keys.T, preferred_element_type=jnp.float32) * factor  24.7 us
    dot_general x10, matrix products, one_block(): jnp.dot(weights, values, preferred_element_type=jnp.float32)  23.8 us
    reduce_sum x10, other arithmetic, one_block(): weights = (expo / jnp.sum(expo, axis=1, keepdims=True)).astype(jnp.bfloat16)  11.3 us
    all_to_all x1, waiting for transfers between devices, body(): lax.all_to_all(k_main, 'seq', split_axis=1, concat_axis=0, tiled=True)  10.6 us
  transfers between devices with their start and end apart: 10, of which 7 were waited for; matrix products, arithmetic and copies ran while one was open for 19% of the time, Pallas kernels for 0%

commit v1 on v0

v1 whole, which is shorter than its diff:
```python
import math

import jax
import jax.numpy as jnp
from jax import lax
from jax.experimental import pallas as pl
from jax.experimental.pallas import tpu as pltpu
from jax.sharding import PartitionSpec as P

HEADS = 32
HEAD_DIM = 128
WIDTH = 4096
TOK_DEV = 128
CTRL_DEV = 32
FRAMES = 8
LEVELS = 16
SEQ = 4096
CTRL = 1024
META = 16
ROW_K = 0
ROW_V = TOK_DEV
ROW_M = 2 * TOK_DEV
ROW_C = ROW_M + META
ROWS = ROW_C + 3 * CTRL_DEV
SCALE = 1.0 / math.sqrt(HEAD_DIM)
SCALE2 = SCALE * math.log2(math.e)
QB = 512
KB = 512
VMEM_LIMIT = 56 * 1024 * 1024
F32 = jnp.float32
BF16 = jnp.bfloat16


def params():
    return pltpu.CompilerParams(vmem_limit_bytes=VMEM_LIMIT)


def rms_round(values, gain):
    wide = values.astype(F32)
    mean_sq = jnp.mean(wide * wide, axis=-1, keepdims=True)
    return (wide * lax.rsqrt(mean_sq + 1e-06) * gain).astype(BF16)


def lay_heads(out_ref, row, values):
    rows = values.shape[0]
    for head in range(HEADS):
        out_ref[head, row : row + rows, :] = values[:, head * HEAD_DIM : (head + 1) * HEAD_DIM]


def pack_kernel(k, v, cq, ck, cv, gk, gcq, gck, meta, out):
    step = 32
    for at in range(0, TOK_DEV, step):
        lay_heads(out, ROW_K + at, rms_round(k[at : at + step, :], gk[...]))
        lay_heads(out, ROW_V + at, v[at : at + step, :])
    lay_heads(out, ROW_C, rms_round(cq[...], gcq[...]))
    lay_heads(out, ROW_C + CTRL_DEV, rms_round(ck[...], gck[...]))
    lay_heads(out, ROW_C + 2 * CTRL_DEV, cv[...])
    for head in range(HEADS):
        out[head, ROW_M : ROW_M + META, :] = meta[...]


def pack_query_kernel(q, gq, out):
    step = 32
    for at in range(0, TOK_DEV, step):
        lay_heads(out, at, rms_round(q[at : at + step, :], gq[...]))


def ctrl_kernel(first, out, held, sem):
    copy = pltpu.make_async_copy(first.at[:, pl.ds(ROW_C, 3 * CTRL_DEV), :], held, sem)
    copy.start()
    copy.wait()
    keys = held[:, CTRL_DEV : 2 * CTRL_DEV, :].reshape(CTRL, HEAD_DIM)
    values = held[:, 2 * CTRL_DEV :, :].reshape(CTRL, HEAD_DIM)
    for part in range(4):
        queries = held[part * 8 : part * 8 + 8, :CTRL_DEV, :].reshape(256, HEAD_DIM)
        scores = lax.dot_general(queries, keys, (((1,), (1,)), ((), ())), preferred_element_type=F32)
        top = jnp.max(scores, axis=1, keepdims=True)
        expo = jnp.exp2((scores - top) * SCALE2)
        total = jnp.sum(expo, axis=1, keepdims=True)
        weights = (expo * (1.0 / total)).astype(BF16)
        out[part * 256 : part * 256 + 256, :] = jnp.dot(
            weights, values, preferred_element_type=F32
        ).astype(BF16)


def main_kernel(places, table, first, query, hint, out, kv, meta, k_t, v_one, acc, top_ref, sems):
    copies = [
        pltpu.make_async_copy(first.at[:, pl.ds(ROW_K, 2 * TOK_DEV), :], kv, sems.at[0]),
        pltpu.make_async_copy(first.at[:, pl.ds(ROW_M, META), :], meta, sems.at[1]),
    ]
    for copy in copies:
        copy.start()
    for copy in copies:
        copy.wait()
    wide_meta = meta[...].astype(F32)
    frames = wide_meta[:, 0, :]
    high = jnp.sum(wide_meta[:, 1, :].reshape(8, 4, 128), axis=1)
    low = jnp.sum(wide_meta[:, 2, :].reshape(8, 4, 128), axis=1)
    match = high * 64.0 + low
    ends = [
        jnp.sum(jnp.where(frames <= f + 0.5, 1.0, 0.0)).astype(jnp.int32) for f in range(FRAMES)
    ]

    def end_of(token):
        end = jnp.int32(SEQ)
        for f in reversed(range(FRAMES)):
            end = jnp.where(ends[f] > token, ends[f], end)
        return end

    for block in range(HEADS):
        k_t[:, block * 128 : block * 128 + 128] = (
            kv[block, :TOK_DEV, :].astype(F32).T.astype(BF16)
        )
        v_one[block * 128 : block * 128 + 128, :HEAD_DIM] = kv[block, TOK_DEV:, :]
    v_one[:, HEAD_DIM:] = jnp.ones((SEQ, HEAD_DIM), BF16)

    def one_block(i, carry):
        base = i * QB
        queries = query[pl.ds(i * (QB // TOK_DEV), QB // TOK_DEV), :, :].reshape(QB, HEAD_DIM)
        n_full = end_of(base) // KB
        n_all = (end_of(base + QB - 1) + KB - 1) // KB
        token = lax.broadcasted_iota(jnp.int32, (QB, 128), 0) + base
        limit = jnp.full((QB, 128), SEQ, jnp.int32)
        for f in reversed(range(FRAMES)):
            limit = jnp.where(ends[f] > token, ends[f], limit)
        acc[...] = jnp.zeros_like(acc)
        top_ref[...] = jnp.full_like(top_ref, -1e30)

        def step(j, masked):
            at = pl.multiple_of(j * KB, KB)
            scores = jnp.dot(queries, k_t[:, pl.ds(at, KB)], preferred_element_type=F32)
            if masked:
                column = lax.broadcasted_iota(jnp.int32, (QB, KB), 1) + at
                scores = jnp.where(column < limit[:, :1], scores, -1e30)
            old = top_ref[...]
            new = jnp.maximum(old, jnp.max(scores, axis=1, keepdims=True))
            top_ref[...] = new
            expo = jnp.exp2((scores - new[:, :1]) * SCALE2).astype(BF16)
            part = jnp.dot(expo, v_one[pl.ds(at, KB), :], preferred_element_type=F32)
            back = jnp.exp2((old - new) * SCALE2)
            acc[:, :HEAD_DIM] = acc[:, :HEAD_DIM] * back + part[:, :HEAD_DIM]
            acc[:, HEAD_DIM:] = acc[:, HEAD_DIM:] * back + part[:, HEAD_DIM:]

        @pl.loop(0, n_full)
        def _(j):
            step(j, False)

        @pl.loop(n_full, n_all)
        def _(j):
            step(j, True)

        attn = (acc[:, :HEAD_DIM] / acc[:, HEAD_DIM:]).astype(BF16).astype(F32)
        gate = jnp.broadcast_to(table[pl.ds(places[1], 1), :], (QB, HEAD_DIM))
        for f in range(1, FRAMES):
            gate = jnp.where(token >= ends[f - 1], table[pl.ds(places[1 + f], 1), :], gate)
        spot = token.astype(F32)
        picks = jnp.concatenate(
            [jnp.where(spot == match[g : g + 1, :], 1.0, 0.0).astype(BF16) for g in range(8)], axis=1
        )
        added = jnp.dot(picks, hint[...], preferred_element_type=F32)
        mixed = (gate * attn + added).astype(BF16)
        out[pl.ds(i * (QB // TOK_DEV), QB // TOK_DEV), :, :] = mixed.reshape(
            QB // TOK_DEV, TOK_DEV, HEAD_DIM
        )
        return carry

    lax.fori_loop(0, SEQ // QB, one_block, 0)


def whole():
    return pl.BlockSpec(memory_space=pltpu.VMEM)


def exchange(block):
    return lax.all_to_all(block, "seq", split_axis=0, concat_axis=0, tiled=True)


def body(
    query,
    key,
    value,
    gain_query,
    gain_key,
    ctrl_query,
    ctrl_key,
    ctrl_value,
    ctrl_gain_query,
    ctrl_gain_key,
    gate_table,
    levels,
    frame_map,
    control_match,
):
    here = lax.axis_index("seq")
    lane = jnp.arange(128, dtype=jnp.int32)
    spread = jnp.where(lane // CTRL_DEV == here % 4, jnp.tile(control_match[0], 4), 0)
    meta = jnp.concatenate(
        [
            frame_map,
            (spread // 64)[None],
            (spread % 64)[None],
            jnp.zeros((META - 3, 128), jnp.int32),
        ],
        axis=0,
    ).astype(BF16)
    packed = pl.pallas_call(
        pack_kernel,
        out_shape=jax.ShapeDtypeStruct((HEADS, ROWS, HEAD_DIM), BF16),
        in_specs=[whole()] * 9,
        out_specs=whole(),
        compiler_params=params(),
        cost_estimate=pl.CostEstimate(flops=8_000_000, bytes_accessed=6_000_000, transcendentals=0),
        name="pack",
    )(
        key[0],
        value[0],
        ctrl_query[0],
        ctrl_key[0],
        ctrl_value[0],
        gain_key[None],
        ctrl_gain_query[None],
        ctrl_gain_key[None],
        meta,
    )
    first = exchange(packed)
    packed_query = pl.pallas_call(
        pack_query_kernel,
        out_shape=jax.ShapeDtypeStruct((HEADS, TOK_DEV, HEAD_DIM), BF16),
        in_specs=[whole()] * 2,
        out_specs=whole(),
        compiler_params=params(),
        cost_estimate=pl.CostEstimate(flops=4_000_000, bytes_accessed=2_000_000, transcendentals=0),
        name="pack_query",
    )(query[0], gain_query[None])
    second = exchange(packed_query)
    hint = pl.pallas_call(
        ctrl_kernel,
        out_shape=jax.ShapeDtypeStruct((CTRL, HEAD_DIM), BF16),
        in_specs=[pl.BlockSpec(memory_space=pl.ANY)],
        out_specs=whole(),
        scratch_shapes=[
            pltpu.VMEM((HEADS, 3 * CTRL_DEV, HEAD_DIM), BF16),
            pltpu.SemaphoreType.DMA,
        ],
        compiler_params=params(),
        cost_estimate=pl.CostEstimate(
            flops=4 * CTRL * CTRL * HEAD_DIM, bytes_accessed=1_000_000, transcendentals=CTRL * CTRL
        ),
        name="ctrl_attention",
    )(first)
    groups = lax.axis_size("grp")
    hint = lax.ppermute(hint, "grp", [((i - 1) % groups, i) for i in range(groups)])
    places = jnp.concatenate([here[None].astype(jnp.int32), levels[0]])
    mixed = pl.pallas_call(
        main_kernel,
        grid_spec=pltpu.PrefetchScalarGridSpec(
            num_scalar_prefetch=1,
            grid=(1,),
            in_specs=[
                pl.BlockSpec((LEVELS, HEAD_DIM), lambda i, places: (0, places[0])),
                pl.BlockSpec(memory_space=pl.ANY),
                whole(),
                whole(),
            ],
            out_specs=whole(),
            scratch_shapes=[
                pltpu.VMEM((HEADS, 2 * TOK_DEV, HEAD_DIM), BF16),
                pltpu.VMEM((HEADS, META, HEAD_DIM), BF16),
                pltpu.VMEM((HEAD_DIM, SEQ), BF16),
                pltpu.VMEM((SEQ, 2 * HEAD_DIM), BF16),
                pltpu.VMEM((QB, 2 * HEAD_DIM), F32),
                pltpu.VMEM((QB, HEAD_DIM), F32),
                pltpu.SemaphoreType.DMA((2,)),
            ],
        ),
        out_shape=jax.ShapeDtypeStruct((HEADS, TOK_DEV, HEAD_DIM), BF16),
        compiler_params=params(),
        cost_estimate=pl.CostEstimate(
            flops=4 * SEQ * SEQ * HEAD_DIM, bytes_accessed=5_000_000, transcendentals=SEQ * SEQ
        ),
        name="main_attention",
    )(places, gate_table, first, second, hint)
    back = exchange(mixed)
    return jnp.swapaxes(back, 0, 1).reshape(1, TOK_DEV, WIDTH)


def solution(mesh):
    return jax.shard_map(
        body,
        mesh=mesh,
        in_specs=(
            P("grp", "seq", None),
            P("grp", "seq", None),
            P("grp", "seq", None),
            P(),
            P(),
            P("grp", "seq", None),
            P("grp", "seq", None),
            P("grp", "seq", None),
            P(),
            P(),
            P(),
            P("grp", None),
            P("grp", "seq"),
            P("grp", "seq"),
        ),
        out_specs=P("grp", "seq", None),
        check_vma=False,
    )
```

time: 400 us -> 151 us (0.38)
  blocking collectives: 108 us -> 22.9 us
  waiting for transfers between devices: 125 us -> 47 us
  Pallas kernels: 0 us -> 57.9 us
  matrix products: 50.7 us -> 0 us
  other arithmetic: 46.1 us -> 1.98 us
  starting transfers between devices: 38.6 us -> 15.8 us
  between operations: 14.5 us -> 0.08 us
  local copies, waits for them, and re-layouts: 16 us -> 3.49 us
    all_gather x1 -> x0, blocking collectives: 81.1 us -> none  [body(): frames_all = lax.all_gather(frames_local, 'seq', axis=0, tiled=True)]
    all_gather x1 -> x0, waiting for transfers between devices: 74.5 us -> none  [body(): rows_in = lax.all_gather(hint_rows, 'seq', axis=0, tiled=True)]
    pallas_call x0 -> x4, Pallas kernels: none -> 57.9 us  [the longest x1 46.3 us: body(): pl.pallas_call(main_kernel, grid_spec=pltpu.PrefetchScalarGridSpec(num_sc...]
    dot_general x21 -> x0, matrix products: 50.7 us -> none  [the longest x10 24.7 us: one_block(): scores = jnp.dot(part, keys.T, preferred_element_type=jnp.float32) * factor]
    unnamed x1 -> x0, blocking collectives: 27 us -> none
    scatter-add x1 -> x0, other arithmetic: 25.4 us -> none  [body(): added = empty.at[target].add(rows_in.astype(jnp.float32), mode='drop')]
    all_to_all x0 -> x1, blocking collectives: none -> 22.9 us  [exchange(): return lax.all_to_all(block, 'seq', split_axis=0, concat_axis=0, tiled=True)]
    all_to_all x8 -> x2, starting transfers between devices: 38.5 us -> 15.7 us  [exchange(): return lax.all_to_all(block, 'seq', split_axis=0, concat_axis=0, tiled=True)]
  transfers between devices with their start and end apart: 10 -> 3, of which waited for: 7 -> 2; matrix products, arithmetic and copies ran while one was open for 19% -> 0% of each run, Pallas kernels for 0% -> 5%
where the time goes in v1:
time: 151 us; the launch traced here: 149 us
  Pallas kernels  57.9 us (38%)
  waiting for transfers between devices  47 us (31%)
  blocking collectives  22.9 us (15%)
  starting transfers between devices  15.8 us (10%)
  local copies, waits for them, and re-layouts  3.49 us (2%)
  other arithmetic  1.98 us (1%)
    all_to_all x2, waiting for transfers between devices, exchange(): return lax.all_to_all(block, 'seq', split_axis=0, concat_axis=0, tiled=True)  47 us
    pallas_call x1, Pallas kernels, body(): pl.pallas_call(main_kernel, grid_spec=pltpu.PrefetchScalarGridSpec(num_sc...  46.3 us
    all_to_all x1, blocking collectives, exchange(): return lax.all_to_all(block, 'seq', split_axis=0, concat_axis=0, tiled=True)  22.9 us
    all_to_all x2, starting transfers between devices, exchange(): return lax.all_to_all(block, 'seq', split_axis=0, concat_axis=0, tiled=True)  15.7 us
    pallas_call x1, Pallas kernels, body(): pl.pallas_call(pack_kernel, out_shape=jax.ShapeDtypeStruct((HEADS, ROWS,...  4.44 us
    pallas_call x1, Pallas kernels, body(): pl.pallas_call(ctrl_kernel, out_shape=jax.ShapeDtypeStruct((CTRL, HEAD_DI...  4.42 us
  transfers between devices with their start and end apart: 3, of which 2 were waited for; matrix products, arithmetic and copies ran while one was open for 0% of the time, Pallas kernels for 5%

profile of v1, /device:TPU:64, one launch (start us, length us, event | category | flops | bytes accessed | tf_op | source)
XLA Modules:
  0.0 149.2 jit_solution(18293910685512316266)
XLA Ops:
  0.0 0.7 tile.11
  0.7 0.1 tile.12
  0.8 0.7 convert.11
  1.4 0.1 pad.3.clone
  1.5 0.7 maximum_maximum_fusion.meta
  2.2 4.4 %pack.1 = bf16[32,368,128]{2,1,0:T(8,128)(2,1)} custom-call(bf16[128,4096]{1,0:T(8,128)(2,1)} %bitcast.17, bf16[128,4096]{1,0:T(8,128)(2,1)} %bitcast.18, bf16[32,4096]{1,0:T(8,128)(2,1)} %bitcast.20, bf16[32,4096]{1,0:T(8,128)(2,1)} %bitcast.21, bf16[32,4096]{1,0:T(8,128)(2,1)} %bitcast.22, f32[1,4096]{1,0:T(1,128)} %bitcast.23, f32[1,4096]{1,0:T(1,128)} %bitcast.24, ...), custom_call_target="tpu_custom_call" | custom-call | flops 8000000 | bytes 6000000 | tf_op jit(solution)/shard_map/pack/pallas_call | solution.py:206
  6.6 8.4 %all-to-all-start = ((bf16[32,368,128]{2,1,0:T(8,128)(2,1)}), bf16[32,368,128]{2,1,0:T(8,128)(2,1)S(1)}, u32[]{:S(2)}, u32[]{:S(2)}) async-start(bf16[32,368,128]{2,1,0:T(8,128)(2,1)} %pack.1), calls=%async_computation | async-start | bytes 6029312 | tf_op jit(solution)/shard_map/all_to_all | solution.py:175
  15.0 2.8 %pack_query.1 = bf16[32,128,128]{2,1,0:T(8,128)(2,1)} custom-call(bf16[128,4096]{1,0:T(8,128)(2,1)} %bitcast.19, f32[1,4096]{1,0:T(1,128)} %bitcast.26), custom_call_target="tpu_custom_call" | custom-call | flops 4000000 | bytes 2000000 | tf_op jit(solution)/shard_map/pack_query/pallas_call | solution.py:226
  17.8 0.0 copy-start.2
  17.8 35.2 %all-to-all-done.first = bf16[32,368,128]{2,1,0:T(8,128)(2,1)S(1)} async-done(((bf16[32,368,128]{2,1,0:T(8,128)(2,1)}), bf16[32,368,128]{2,1,0:T(8,128)(2,1)S(1)}, u32[]{:S(2)}, u32[]{:S(2)}) %all-to-all-start) | async-done | bytes 3014688 | tf_op jit(solution)/shard_map/all_to_all | solution.py:175
  52.9 0.0 copy-start
  52.9 7.3 %all-to-all-start.1 = ((bf16[32,128,128]{2,1,0:T(8,128)(2,1)}), bf16[32,128,128]{2,1,0:T(8,128)(2,1)}, u32[]{:S(2)}, u32[]{:S(2)}) async-start(bf16[32,128,128]{2,1,0:T(8,128)(2,1)} %pack_query.1), calls=%async_computation.1 | async-start | bytes 2097152 | tf_op jit(solution)/shard_map/all_to_all | solution.py:175
  60.3 0.0 copy-done
  60.3 4.4 %ctrl_attention.1 = bf16[1024,128]{1,0:T(8,128)(2,1)} custom-call(bf16[32,368,128]{2,1,0:T(8,128)(2,1)} %copy-done), custom_call_target="tpu_custom_call" | custom-call | flops 536870912 | bytes 1000000 | tf_op jit(solution)/shard_map/ctrl_attention/pallas_call | solution.py:236
  64.7 0.1 collective-permute-start
  64.8 0.0 copy-done.2
  64.8 0.6 pad_add_fusion.places
  65.4 11.9 %all-to-all-done.1.query = bf16[32,128,128]{2,1,0:T(8,128)(2,1)} async-done(((bf16[32,128,128]{2,1,0:T(8,128)(2,1)}), bf16[32,128,128]{2,1,0:T(8,128)(2,1)}, u32[]{:S(2)}, u32[]{:S(2)}) %all-to-all-start.1) | async-done | bytes 1048608 | tf_op jit(solution)/shard_map/all_to_all | solution.py:175
  77.3 0.0 collective-permute-done.hint
  77.3 0.0 copy-start.1
  77.3 0.7 copy-done.1
  78.0 46.3 %main_attention.1 = bf16[32,128,128]{2,1,0:T(8,128)(2,1)} custom-call(s32[9]{0:T(128)} %pad_add_fusion.places, f32[16,4096]{1,0:T(8,128)} %table.1, bf16[32,368,128]{2,1,0:T(8,128)(2,1)} %copy-done, bf16[32,128,128]{2,1,0:T(8,128)(2,1)} %all-to-all-done.1.query, bf16[1024,128]{1,0:T(8,128)(2,1)} %copy-done.1), custom_call_target="tpu_custom_call" | custom-call | flops 8589934592 | bytes 5000000 | tf_op jit(solution)/shard_map/main_attention/pallas_call | solution.py:254
  124.3 22.9 %all_to_all.15 = bf16[32,128,128]{2,1,0:T(8,128)(2,1)S(1)} all-to-all(bf16[32,128,128]{2,1,0:T(8,128)(2,1)} %main_attention.1), channel_id=1, replica_groups=mesh['grp'=4,'seq'=32] {'seq'}, dimensions={0} | all-to-all | bytes 2097152 | tf_op jit(solution)/shard_map/all_to_all | solution.py:175
  147.2 0.7 copy.15
  147.8 1.3 copy.16
  (3 shorter events, 0.0 us)
Async XLA Ops:
  6.6 46.3 %all-to-all-start = ((bf16[32,368,128]{2,1,0:T(8,128)(2,1)}), bf16[32,368,128]{2,1,0:T(8,128)(2,1)S(1)}, u32[]{:S(2)}, u32[]{:S(2)}) async-start(bf16[32,368,128]{2,1,0:T(8,128)(2,1)} %pack.1), calls=%async_computation | async-start | bytes 6029312 | tf_op jit(solution)/shard_map/all_to_all | solution.py:175
  17.8 47.0 %copy-start.2 = (s32[1,8]{1,0:T(1,128)S(1)}, s32[1,8]{1,0:T(1,128)}, u32[]{:S(2)}) copy-start(s32[1,8]{1,0:T(1,128)} %param.25) | copy-start | bytes 100
  52.9 7.4 %copy-start = (bf16[32,368,128]{2,1,0:T(8,128)(2,1)}, bf16[32,368,128]{2,1,0:T(8,128)(2,1)S(1)}, u32[]{:S(2)}) copy-start(bf16[32,368,128]{2,1,0:T(8,128)(2,1)S(1)} %all-to-all-done.first) | copy-start | bytes 9043972
  52.9 24.4 %all-to-all-start.1 = ((bf16[32,128,128]{2,1,0:T(8,128)(2,1)}), bf16[32,128,128]{2,1,0:T(8,128)(2,1)}, u32[]{:S(2)}, u32[]{:S(2)}) async-start(bf16[32,128,128]{2,1,0:T(8,128)(2,1)} %pack_query.1), calls=%async_computation.1 | async-start | bytes 2097152 | tf_op jit(solution)/shard_map/all_to_all | solution.py:175
  64.7 12.6 %collective-permute-start = (bf16[1024,128]{1,0:T(8,128)(2,1)}, bf16[1024,128]{1,0:T(8,128)(2,1)S(1)}, u32[]{:S(2)}, u32[]{:S(2)}) collective-permute-start(bf16[1024,128]{1,0:T(8,128)(2,1)} %ctrl_attention.1), channel_id=1, source_target_pairs={{96,0},{0,32},{32,64},{64,96},{97,1},{1,33},{33,65},{65,97},{98,2}... | collective-permute-start | bytes 786440 | tf_op jit(solution)/shard_map/ppermute | solution.py:252
  77.3 0.7 copy-start.1

commit v2 on v1

v2 whole, which is shorter than its diff:
```python
import math

import jax
import jax.numpy as jnp
from jax import lax
from jax.experimental import pallas as pl
from jax.experimental.pallas import tpu as pltpu
from jax.sharding import PartitionSpec as P

HEADS = 32
HEAD_DIM = 128
WIDTH = 4096
TOK_DEV = 128
CTRL_DEV = 32
FRAMES = 8
LEVELS = 16
SEQ = 4096
CTRL = 1024
META = 16
ROW_M = 3 * CTRL_DEV
ROWS_C = ROW_M + META
ROWS = 3 * TOK_DEV
SCALE2 = math.log2(math.e) / math.sqrt(HEAD_DIM)
QB = 512
KB = 1024
VR = HEAD_DIM + 16
SAFE = 2.0**100
VMEM_LIMIT = 20 * 1024 * 1024
F32 = jnp.float32
BF16 = jnp.bfloat16


def params():
    return pltpu.CompilerParams(vmem_limit_bytes=VMEM_LIMIT)


def whole():
    return pl.BlockSpec(memory_space=pltpu.VMEM)


def rms_round(values, gain):
    wide = values.astype(F32)
    mean_sq = jnp.mean(wide * wide, axis=-1, keepdims=True)
    return (wide * lax.rsqrt(mean_sq + 1e-06) * gain).astype(BF16)


def lay_heads(out_ref, row, values):
    rows = values.shape[0]
    for head in range(HEADS):
        out_ref[head, row : row + rows, :] = values[:, head * HEAD_DIM : (head + 1) * HEAD_DIM]


def pack_ctrl_kernel(cq, ck, cv, gcq, gck, frames, match, out):
    lay_heads(out, 0, rms_round(cq[...], gcq[...]))
    lay_heads(out, CTRL_DEV, rms_round(ck[...], gck[...]))
    lay_heads(out, 2 * CTRL_DEV, cv[...])
    spots = jnp.concatenate([match[...]] * 4, axis=1)
    row = lax.broadcasted_iota(jnp.int32, (META, 128), 0)
    meta = jnp.where(row == 0, frames[...], jnp.where(row == 1, spots // 64, spots % 64))
    meta = jnp.where(row < 3, meta, 0).astype(F32).astype(BF16)
    for head in range(HEADS):
        out[head, ROW_M:, :] = meta


def pack_main_kernel(q, k, v, gq, gk, out):
    step = 32
    for at in range(0, TOK_DEV, step):
        lay_heads(out, at, rms_round(q[at : at + step, :], gq[...]))
        lay_heads(out, TOK_DEV + at, rms_round(k[at : at + step, :], gk[...]))
        lay_heads(out, 2 * TOK_DEV + at, v[at : at + step, :])


def ctrl_kernel(first, hint, ends):
    frames = first[:, ROW_M:, :].astype(F32)[:, 0, :]
    for f in range(FRAMES):
        ends[f] = jnp.sum(jnp.where(frames <= f + 0.5, 1.0, 0.0)).astype(jnp.int32)
    keys = first[:, CTRL_DEV : 2 * CTRL_DEV, :].reshape(CTRL, HEAD_DIM)
    values = first[:, 2 * CTRL_DEV : ROW_M, :].reshape(CTRL, HEAD_DIM)
    for part in range(4):
        queries = first[part * 8 : part * 8 + 8, :CTRL_DEV, :].reshape(256, HEAD_DIM)
        scores = lax.dot_general(queries, keys, (((1,), (1,)), ((), ())), preferred_element_type=F32)
        top = jnp.max(scores, axis=1, keepdims=True)
        expo = jnp.exp2((scores - top) * SCALE2)
        total = jnp.sum(expo, axis=1, keepdims=True)
        weights = (expo * (1.0 / total)).astype(BF16)
        hint[part * 256 : part * 256 + 256, :] = jnp.dot(
            weights, values, preferred_element_type=F32
        ).astype(BF16)


def place_kernel(places, table, first, hint, added, gates):
    for f in range(FRAMES):
        gates[f : f + 1, :] = table[pl.ds(places[1 + f], 1), :]
    meta = first[:, ROW_M:, :].astype(F32)
    spots = (meta[:, 1, :] * 64.0 + meta[:, 2, :]).reshape(8, 4, 128)
    source = lax.broadcasted_iota(jnp.int32, (8, 4, 128), 1)
    lane = lax.broadcasted_iota(jnp.int32, (8, 4, 128), 2)
    match = jnp.sum(jnp.where(lane // CTRL_DEV == source, spots, 0.0), axis=1)
    for i in range(SEQ // QB):
        spot = (lax.broadcasted_iota(jnp.int32, (QB, 128), 0) + i * QB).astype(F32)
        picks = jnp.concatenate(
            [jnp.where(spot == match[g : g + 1, :], 1.0, 0.0).astype(BF16) for g in range(8)], axis=1
        )
        rows = jnp.dot(picks, hint[...], preferred_element_type=F32).astype(BF16)
        added[i * (QB // TOK_DEV) : (i + 1) * (QB // TOK_DEV), :, :] = rows.reshape(
            QB // TOK_DEV, TOK_DEV, HEAD_DIM
        )


def main_kernel(ends_ref, gates, second, added, out, v_t, acc, sums, top_ref):
    ends = [ends_ref[f] for f in range(FRAMES)]

    def end_of(token):
        end = jnp.int32(SEQ)
        for f in reversed(range(FRAMES)):
            end = jnp.where(ends[f] > token, ends[f], end)
        return end

    for block in range(HEADS):
        v_t[:HEAD_DIM, block * 128 : block * 128 + 128] = (
            second[block, 2 * TOK_DEV :, :].astype(F32).T.astype(BF16)
        )
    v_t[HEAD_DIM:, :] = jnp.ones((VR - HEAD_DIM, SEQ), BF16)

    def limit_of(base):
        column = lax.broadcasted_iota(jnp.int32, (8, QB), 1) + base
        limit = jnp.full((8, QB), SEQ, jnp.int32)
        for f in reversed(range(FRAMES)):
            limit = jnp.where(ends[f] > column, ends[f], limit)
        return limit[:1, :]

    def scores_of(i, j, masked):
        queries = second[pl.ds(i * (QB // TOK_DEV), QB // TOK_DEV), :TOK_DEV, :]
        q_t = queries.reshape(QB, HEAD_DIM).astype(F32).T.astype(BF16)
        keys = second[pl.ds(j * (KB // TOK_DEV), KB // TOK_DEV), TOK_DEV : 2 * TOK_DEV, :]
        scores = jnp.dot(keys.reshape(KB, HEAD_DIM), q_t, preferred_element_type=F32)
        return scores

    def visible(limit, j):
        return lax.broadcasted_iota(jnp.int32, (KB, QB), 0) < limit - j * KB

    def values_of(j):
        return v_t[:, pl.ds(pl.multiple_of(j * KB, KB), KB)]

    def finish(i, total):
        base = i * QB
        token = lax.broadcasted_iota(jnp.int32, (QB, HEAD_DIM), 0) + base
        attn = (total[:HEAD_DIM, :] / total[HEAD_DIM : HEAD_DIM + 1, :]).T.astype(BF16).astype(F32)
        gate = jnp.broadcast_to(gates[0:1, :], (QB, HEAD_DIM))
        for f in range(1, FRAMES):
            gate = jnp.where(token >= ends[f - 1], gates[f : f + 1, :], gate)
        at = pl.ds(i * (QB // TOK_DEV), QB // TOK_DEV)
        rows = added[at, :, :].reshape(QB, HEAD_DIM).astype(F32)
        out[at, :, :] = (gate * attn + rows).astype(BF16).reshape(QB // TOK_DEV, TOK_DEV, HEAD_DIM)

    def quick_block(i, carry):
        base = i * QB
        n_full = end_of(base) // KB
        n_all = (end_of(base + QB - 1) + KB - 1) // KB
        limit = limit_of(base)
        queries = second[pl.ds(i * (QB // TOK_DEV), QB // TOK_DEV), :TOK_DEV, :]
        q_t = queries.reshape(QB, HEAD_DIM).astype(F32).T.astype(BF16)
        acc[...] = jnp.zeros_like(acc)

        def step(j, masked):
            keys = second[pl.ds(j * (KB // TOK_DEV), KB // TOK_DEV), TOK_DEV : 2 * TOK_DEV, :]
            scores = jnp.dot(keys.reshape(KB, HEAD_DIM), q_t, preferred_element_type=F32)
            expo = jnp.exp2(scores * SCALE2)
            if masked:
                expo = jnp.where(visible(limit, j), expo, 0.0)
            acc[...] += jnp.dot(values_of(j), expo.astype(BF16), preferred_element_type=F32)

        @pl.loop(0, n_full)
        def _(j):
            step(j, False)

        @pl.loop(n_full, n_all)
        def _(j):
            step(j, True)

        sums[pl.ds(i, 1), :] = acc[HEAD_DIM : HEAD_DIM + 1, :]
        finish(i, acc)
        return carry

    def full_block(i, carry):
        base = i * QB
        n_all = (end_of(base + QB - 1) + KB - 1) // KB
        limit = limit_of(base)
        acc[...] = jnp.zeros_like(acc)
        top_ref[...] = jnp.full_like(top_ref, -1e30)

        @pl.loop(0, n_all)
        def _(j):
            scores = jnp.where(visible(limit, j), scores_of(i, j, True), -1e30)
            old = top_ref[:1, :]
            new = jnp.maximum(old, jnp.max(scores, axis=0, keepdims=True))
            expo = jnp.exp2((scores - new) * SCALE2).astype(BF16)
            part = jnp.dot(values_of(j), expo, preferred_element_type=F32)
            acc[...] = acc[...] * jnp.exp2((old - new) * SCALE2) + part
            top_ref[...] = jnp.broadcast_to(new, top_ref.shape)

        finish(i, acc)
        return carry

    lax.fori_loop(0, SEQ // QB, quick_block, 0)
    good = (sums[...] > 1.0 / SAFE) & (sums[...] < SAFE)
    count = jnp.sum(jnp.where(good, 1.0, 0.0))

    @pl.when(count < SEQ - 0.5)
    def _():
        lax.fori_loop(0, SEQ // QB, full_block, 0)


def unpack_kernel(rows, out):
    for head in range(HEADS):
        out[:, head * HEAD_DIM : (head + 1) * HEAD_DIM] = rows[head, :, :]


def cost(flops, moved, transcendentals=0):
    return pl.CostEstimate(flops=flops, bytes_accessed=moved, transcendentals=transcendentals)


def shape(*dims, dtype=BF16):
    return jax.ShapeDtypeStruct(dims, dtype)


def run_main(ends, gates, second, added):
    return pl.pallas_call(
        main_kernel,
        out_shape=shape(HEADS, TOK_DEV, HEAD_DIM),
        in_specs=[pl.BlockSpec(memory_space=pltpu.SMEM), whole(), whole(), whole()],
        out_specs=whole(),
        scratch_shapes=[
            pltpu.VMEM((VR, SEQ), BF16),
            pltpu.VMEM((VR, QB), F32),
            pltpu.VMEM((SEQ // QB, QB), F32),
            pltpu.VMEM((8, QB), F32),
        ],
        compiler_params=params(),
        cost_estimate=cost(4 * SEQ * SEQ * HEAD_DIM, 5_000_000, SEQ * SEQ),
        name="main_attention",
    )(ends, gates, second, added)


def exchange(block):
    return lax.all_to_all(block, "seq", split_axis=0, concat_axis=0, tiled=True)


def body(
    query,
    key,
    value,
    gain_query,
    gain_key,
    ctrl_query,
    ctrl_key,
    ctrl_value,
    ctrl_gain_query,
    ctrl_gain_key,
    gate_table,
    levels,
    frame_map,
    control_match,
):
    packed = pl.pallas_call(
        pack_ctrl_kernel,
        out_shape=shape(HEADS, ROWS_C, HEAD_DIM),
        in_specs=[whole()] * 7,
        out_specs=whole(),
        compiler_params=params(),
        cost_estimate=cost(2_000_000, 2_000_000),
        name="pack_ctrl",
    )(
        ctrl_query[0],
        ctrl_key[0],
        ctrl_value[0],
        ctrl_gain_query[None],
        ctrl_gain_key[None],
        frame_map,
        control_match,
    )
    first = exchange(packed)
    packed_main = pl.pallas_call(
        pack_main_kernel,
        out_shape=shape(HEADS, ROWS, HEAD_DIM),
        in_specs=[whole()] * 5,
        out_specs=whole(),
        compiler_params=params(),
        cost_estimate=cost(8_000_000, 6_000_000),
        name="pack_main",
    )(query[0], key[0], value[0], gain_query[None], gain_key[None])
    second = exchange(packed_main)
    hint, ends = pl.pallas_call(
        ctrl_kernel,
        out_shape=(shape(CTRL, HEAD_DIM), shape(FRAMES, dtype=jnp.int32)),
        in_specs=[whole()],
        out_specs=(whole(), pl.BlockSpec(memory_space=pltpu.SMEM)),
        compiler_params=params(),
        cost_estimate=cost(4 * CTRL * CTRL * HEAD_DIM, 1_000_000, CTRL * CTRL),
        name="ctrl_attention",
    )(first)
    groups = lax.axis_size("grp")
    hint = lax.ppermute(hint, "grp", [((i - 1) % groups, i) for i in range(groups)])
    places = jnp.concatenate([lax.axis_index("seq")[None].astype(jnp.int32), levels[0]])
    added, gates = pl.pallas_call(
        place_kernel,
        grid_spec=pltpu.PrefetchScalarGridSpec(
            num_scalar_prefetch=1,
            grid=(1,),
            in_specs=[
                pl.BlockSpec((LEVELS, HEAD_DIM), lambda i, places: (0, places[0])),
                whole(),
                whole(),
            ],
            out_specs=(whole(), whole()),
        ),
        out_shape=(shape(HEADS, TOK_DEV, HEAD_DIM), shape(FRAMES, HEAD_DIM, dtype=F32)),
        compiler_params=params(),
        cost_estimate=cost(2 * SEQ * CTRL * HEAD_DIM, 2_000_000),
        name="place_hints",
    )(places, gate_table, first, hint)
    mixed = run_main(ends, gates, second, added)
    back = exchange(mixed)
    return pl.pallas_call(
        unpack_kernel,
        out_shape=shape(TOK_DEV, WIDTH),
        in_specs=[whole()],
        out_specs=whole(),
        compiler_params=params(),
        cost_estimate=cost(0, 2_000_000),
        name="unpack",
    )(back)[None]


def solution(mesh):
    return jax.shard_map(
        body,
        mesh=mesh,
        in_specs=(
            P("grp", "seq", None),
            P("grp", "seq", None),
            P("grp", "seq", None),
            P(),
            P(),
            P("grp", "seq", None),
            P("grp", "seq", None),
            P("grp", "seq", None),
            P(),
            P(),
            P(),
            P("grp", None),
            P("grp", "seq"),
            P("grp", "seq"),
        ),
        out_specs=P("grp", "seq", None),
        check_vma=False,
    )
```

time: 151 us -> 152 us (level); the launches traced: 149 us -> 152 us
  blocking collectives: 22.9 us -> 53.2 us
  Pallas kernels: 57.9 us -> 33.8 us
  local copies, waits for them, and re-layouts: 3.49 us -> 7.95 us
  starting transfers between devices: 15.8 us -> 12.9 us
  waiting for transfers between devices: 47 us -> 44.3 us
  other arithmetic: 1.98 us -> 0.08 us
    all_to_all x2, waiting for transfers between devices: 47 us -> 12.4 us  [exchange(): return lax.all_to_all(block, 'seq', split_axis=0, concat_axis=0, tiled=True)]
    ppermute x1, waiting for transfers between devices: 0.01 us -> 31.9 us  [body(): lax.ppermute(hint, 'grp', [((i - 1) % groups, i) for i in range(groups)])]
    all_to_all x1, blocking collectives: 22.9 us -> 53.2 us  [exchange(): return lax.all_to_all(block, 'seq', split_axis=0, concat_axis=0, tiled=True)]
    pallas_call x4 -> x6, Pallas kernels: 57.9 us -> 33.8 us  [the longest x1 19.8 us: run_main(): pl.pallas_call(main_kernel, out_shape=shape(HEADS, TOK_DEV, HEAD_DIM), in...]
    unnamed x6 -> x32, local copies, waits for them, and re-layouts: 0.7 us -> 7.95 us
    all_to_all x2, starting transfers between devices: 15.7 us -> 12.8 us  [exchange(): return lax.all_to_all(block, 'seq', split_axis=0, concat_axis=0, tiled=True)]
  transfers between devices with their start and end apart: 3 -> 3, of which waited for: 2 -> 2; matrix products, arithmetic and copies ran while one was open for 0% -> 0% of each run, Pallas kernels for 5% -> 8%
where the time goes in v2:
time: 152 us
  blocking collectives  53.2 us (35%)
  waiting for transfers between devices  44.3 us (29%)
  Pallas kernels  33.8 us (22%)
  starting transfers between devices  12.9 us (8%)
  local copies, waits for them, and re-layouts  7.95 us (5%)
    all_to_all x1, blocking collectives, exchange(): return lax.all_to_all(block, 'seq', split_axis=0, concat_axis=0, tiled=True)  53.2 us
    ppermute x1, waiting for transfers between devices, body(): lax.ppermute(hint, 'grp', [((i - 1) % groups, i) for i in range(groups)])  31.9 us
    pallas_call x1, Pallas kernels, run_main(): pl.pallas_call(main_kernel, out_shape=shape(HEADS, TOK_DEV, HEAD_DIM), in...  19.8 us
    all_to_all x2, starting transfers between devices, exchange(): return lax.all_to_all(block, 'seq', split_axis=0, concat_axis=0, tiled=True)  12.8 us
    all_to_all x2, waiting for transfers between devices, exchange(): return lax.all_to_all(block, 'seq', split_axis=0, concat_axis=0, tiled=True)  12.4 us
    unnamed x32, local copies, waits for them, and re-layouts  7.95 us
    pallas_call x1, Pallas kernels, body(): pl.pallas_call(ctrl_kernel, out_shape=(shape(CTRL, HEAD_DIM), shape(FRAME...  4.49 us
    pallas_call x1, Pallas kernels, body(): pl.pallas_call(place_kernel, grid_spec=pltpu.PrefetchScalarGridSpec(num_s...  4.11 us
  transfers between devices with their start and end apart: 3, of which 2 were waited for; matrix products, arithmetic and copies ran while one was open for 0% of the time, Pallas kernels for 8%

profile of v2, /device:TPU:64, one launch (start us, length us, event | category | flops | bytes accessed | tf_op | source)
XLA Modules:
  0.0 152.3 jit_solution(15497130617088336772)
XLA Ops:
  0.0 0.0 copy-start.2
  0.0 0.0 copy-start.1
  0.0 0.0 copy-start
  0.0 0.0 copy-start.3
  0.0 1.1 copy-done.3
  1.1 0.0 copy-start.4
  1.1 0.9 copy-done.4
  2.1 0.0 copy-start.5
  2.1 0.9 copy-done.5
  3.0 0.0 copy-start.6
  3.0 0.7 copy-done.6
  3.7 0.0 copy-start.7
  3.7 0.7 copy-done.7
  4.4 0.0 copy-start.10
  4.5 0.7 copy-done.10
  5.1 0.0 copy-start.11
  5.1 0.7 copy-done.11
  5.8 0.0 copy-start.8
  5.8 0.0 copy-start.9
  5.8 1.3 pack_ctrl.1
  7.0 8.5 %all-to-all-start = ((bf16[32,112,128]{2,1,0:T(8,128)(2,1)}), bf16[32,112,128]{2,1,0:T(8,128)(2,1)}, u32[]{:S(2)}, u32[]{:S(2)}) async-start(bf16[32,112,128]{2,1,0:T(8,128)(2,1)} %pack_ctrl.1), calls=%async_computation | async-start | bytes 1835008 | tf_op jit(solution)/shard_map/all_to_all | solution.py:246
  15.5 0.0 copy-done.2
  15.5 0.0 copy-done.1
  15.5 0.0 copy-done
  15.6 0.0 copy-done.8
  15.6 0.0 copy-done.9
  15.6 3.0 %pack_main.1 = bf16[32,384,128]{2,1,0:T(8,128)(2,1)} custom-call(bf16[128,4096]{1,0:T(8,128)(2,1)S(1)} %bitcast.13, bf16[128,4096]{1,0:T(8,128)(2,1)S(1)} %bitcast.14, bf16[128,4096]{1,0:T(8,128)(2,1)S(1)} %bitcast.15, f32[1,4096]{1,0:T(1,128)S(1)} %bitcast.21, f32[1,4096]{1,0:T(1,128)S(1)} %bitcast.22), custom_call_target="tpu_custom_call" | custom-call | flops 8000000 | bytes 6000000 | tf_op jit(solution)/shard_map/pack_main/pallas_call | solution.py:283
  18.5 0.0 copy-start.15
  18.5 0.0 copy-start.12
  18.5 12.4 %all-to-all-done.first = bf16[32,112,128]{2,1,0:T(8,128)(2,1)} async-done(((bf16[32,112,128]{2,1,0:T(8,128)(2,1)}), bf16[32,112,128]{2,1,0:T(8,128)(2,1)}, u32[]{:S(2)}, u32[]{:S(2)}) %all-to-all-start) | async-done | bytes 917536 | tf_op jit(solution)/shard_map/all_to_all | solution.py:246
  31.0 4.4 %all-to-all-start.1 = ((bf16[32,384,128]{2,1,0:T(8,128)(2,1)}), bf16[32,384,128]{2,1,0:T(8,128)(2,1)S(1)}, u32[]{:S(2)}, u32[]{:S(2)}) async-start(bf16[32,384,128]{2,1,0:T(8,128)(2,1)} %pack_main.1), calls=%async_computation.1 | async-start | bytes 6291456 | tf_op jit(solution)/shard_map/all_to_all | solution.py:246
  35.3 4.5 %ctrl_attention.1 = (bf16[1024,128]{1,0:T(8,128)(2,1)}, s32[8]{0:T(128)S(1)}) custom-call(bf16[32,112,128]{2,1,0:T(8,128)(2,1)} %all-to-all-done.first), custom_call_target="tpu_custom_call" | custom-call | flops 536870912 | bytes 1000000 | tf_op jit(solution)/shard_map/ctrl_attention/pallas_call | solution.py:293
  39.8 0.1 collective-permute-start
  39.9 0.0 copy-done.15
  39.9 0.1 pad_add_fusion.places
  40.0 31.9 %collective-permute-done.hint = bf16[1024,128]{1,0:T(8,128)(2,1)} collective-permute-done((bf16[1024,128]{1,0:T(8,128)(2,1)}, bf16[1024,128]{1,0:T(8,128)(2,1)}, u32[]{:S(2)}, u32[]{:S(2)}) %collective-permute-start) | collective-permute-done | bytes 262176 | tf_op jit(solution)/shard_map/ppermute | solution.py:303
  71.9 0.0 copy-done.12
  71.9 4.1 %place_hints.1 = (bf16[32,128,128]{2,1,0:T(8,128)(2,1)S(1)}, f32[8,128]{1,0:T(8,128)S(1)}) custom-call(s32[9]{0:T(128)S(1)} %pad_add_fusion.places, f32[16,4096]{1,0:T(8,128)S(1)} %copy-done.12, bf16[32,112,128]{2,1,0:T(8,128)(2,1)} %all-to-all-done.first, bf16[1024,128]{1,0:T(8,128)(2,1)} %collective-permute-done.hint), custom_call_target="tpu_custom_call" | custom-call | flops 1073741824 | bytes 2000000 | tf_op jit(solution)/shard_map/place_hints/pallas_call | solution.py:305
  76.0 0.0 copy-start.13
  76.0 1.0 copy-done.13
  76.9 0.0 all-to-all-done.1.second
  76.9 0.0 copy-start.14
  76.9 1.2 copy-done.14
  78.2 19.8 %main_attention.1 = bf16[32,128,128]{2,1,0:T(8,128)(2,1)S(1)} custom-call(s32[8]{0:T(128)S(1)} %get-tuple-element.9.ends_ref, f32[8,128]{1,0:T(8,128)S(1)} %get-tuple-element.11.gates, bf16[32,384,128]{2,1,0:T(8,128)(2,1)S(1)} %all-to-all-done.1.second, bf16[32,128,128]{2,1,0:T(8,128)(2,1)S(1)} %copy-done.14), custom_call_target="tpu_custom_call" | custom-call | flops 8589934592 | bytes 5000000 | tf_op jit(solution)/shard_map/main_attention/pallas_call | solution.py:228
  97.9 53.2 %all_to_all.15.rows = bf16[32,128,128]{2,1,0:T(8,128)(2,1)S(1)} all-to-all(bf16[32,128,128]{2,1,0:T(8,128)(2,1)S(1)} %main_attention.1), channel_id=1, replica_groups=mesh['grp'=4,'seq'=32] {'seq'}, dimensions={0} | all-to-all | bytes 2097152 | tf_op jit(solution)/shard_map/all_to_all | solution.py:246
  151.1 1.2 unpack.1
Async XLA Ops:
  0.0 15.5 %copy-start.2 = (bf16[1,128,4096]{2,1,0:T(8,128)(2,1)S(1)}, bf16[1,128,4096]{2,1,0:T(8,128)(2,1)}, u32[]{:S(2)}) copy-start(bf16[1,128,4096]{2,1,0:T(8,128)(2,1)} %param.16) | copy-start | bytes 3145732
  0.0 15.5 %copy-start.1 = (bf16[1,128,4096]{2,1,0:T(8,128)(2,1)S(1)}, bf16[1,128,4096]{2,1,0:T(8,128)(2,1)}, u32[]{:S(2)}) copy-start(bf16[1,128,4096]{2,1,0:T(8,128)(2,1)} %param.15) | copy-start | bytes 3145732
  0.0 15.5 %copy-start = (bf16[1,128,4096]{2,1,0:T(8,128)(2,1)S(1)}, bf16[1,128,4096]{2,1,0:T(8,128)(2,1)}, u32[]{:S(2)}) copy-start(bf16[1,128,4096]{2,1,0:T(8,128)(2,1)} %param.14) | copy-start | bytes 3145732
  0.0 1.1 copy-start.3
  1.1 0.9 copy-start.4
  2.1 0.9 copy-start.5
  3.0 0.7 copy-start.6
  3.7 0.7 copy-start.7
  4.4 0.7 copy-start.10
  5.1 0.7 copy-start.11
  5.8 9.8 %copy-start.8 = (f32[4096]{0:T(1024)S(1)}, f32[4096]{0:T(1024)}, u32[]{:S(2)}) copy-start(f32[4096]{0:T(1024)} %param.17) | copy-start | bytes 49156
  5.8 9.8 %copy-start.9 = (f32[4096]{0:T(1024)S(1)}, f32[4096]{0:T(1024)}, u32[]{:S(2)}) copy-start(f32[4096]{0:T(1024)} %param.18) | copy-start | bytes 49156
  7.0 24.0 %all-to-all-start = ((bf16[32,112,128]{2,1,0:T(8,128)(2,1)}), bf16[32,112,128]{2,1,0:T(8,128)(2,1)}, u32[]{:S(2)}, u32[]{:S(2)}) async-start(bf16[32,112,128]{2,1,0:T(8,128)(2,1)} %pack_ctrl.1), calls=%async_computation | async-start | bytes 1835008 | tf_op jit(solution)/shard_map/all_to_all | solution.py:246
  18.5 21.4 %copy-start.15 = (s32[1,8]{1,0:T(1,128)S(1)}, s32[1,8]{1,0:T(1,128)}, u32[]{:S(2)}) copy-start(s32[1,8]{1,0:T(1,128)} %param.25) | copy-start | bytes 100
  18.5 53.3 %copy-start.12 = (f32[16,4096]{1,0:T(8,128)S(1)}, f32[16,4096]{1,0:T(8,128)}, u32[]{:S(2)}) copy-start(f32[16,4096]{1,0:T(8,128)} %table.1) | copy-start | bytes 786436
  31.0 46.0 %all-to-all-start.1 = ((bf16[32,384,128]{2,1,0:T(8,128)(2,1)}), bf16[32,384,128]{2,1,0:T(8,128)(2,1)S(1)}, u32[]{:S(2)}, u32[]{:S(2)}) async-start(bf16[32,384,128]{2,1,0:T(8,128)(2,1)} %pack_main.1), calls=%async_computation.1 | async-start | bytes 6291456 | tf_op jit(solution)/shard_map/all_to_all | solution.py:246
  39.8 32.0 %collective-permute-start = (bf16[1024,128]{1,0:T(8,128)(2,1)}, bf16[1024,128]{1,0:T(8,128)(2,1)}, u32[]{:S(2)}, u32[]{:S(2)}) collective-permute-start(bf16[1024,128]{1,0:T(8,128)(2,1)} %get-tuple-element.10), channel_id=1, source_target_pairs={{96,0},{0,32},{32,64},{64,96},{97,1},{1,33},{33,65},{65,97},{98,2}... | collective-permute-start | bytes 786440 | tf_op jit(solution)/shard_map/ppermute | solution.py:303
  76.0 1.0 copy-start.13
  76.9 1.2 copy-start.14

commit v3 on v2

--- a/solution.py
+++ b/solution.py
@@ -1,3 +1,4 @@
+import functools
 import math
 
 import jax
@@ -23,15 +24,17 @@
 SCALE2 = math.log2(math.e) / math.sqrt(HEAD_DIM)
 QB = 512
 KB = 1024
+PART = 512
+WIDE = 8
 VR = HEAD_DIM + 16
 SAFE = 2.0**100
-VMEM_LIMIT = 20 * 1024 * 1024
+MIB = 1024 * 1024
 F32 = jnp.float32
 BF16 = jnp.bfloat16
 
 
-def params():
-    return pltpu.CompilerParams(vmem_limit_bytes=VMEM_LIMIT)
+def params(mib=20):
+    return pltpu.CompilerParams(vmem_limit_bytes=mib * MIB)
 
 
 def whole():
@@ -70,10 +73,16 @@
         lay_heads(out, 2 * TOK_DEV + at, v[at : at + step, :])
 
 
-def ctrl_kernel(first, hint, ends):
-    frames = first[:, ROW_M:, :].astype(F32)[:, 0, :]
+def ctrl_kernel(places, table, first, hint, ends, notes):
+    meta = first[:, ROW_M:, :].astype(F32)
+    frames = meta[:, 0, :]
     for f in range(FRAMES):
         ends[f] = jnp.sum(jnp.where(frames <= f + 0.5, 1.0, 0.0)).astype(jnp.int32)
+        notes[8 + f : 9 + f, :] = table[pl.ds(places[1 + f], 1), :]
+    spots = (meta[:, 1, :] * 64.0 + meta[:, 2, :]).reshape(8, 4, 128)
+    source = lax.broadcasted_iota(jnp.int32, (8, 4, 128), 1)
+    lane = lax.broadcasted_iota(jnp.int32, (8, 4, 128), 2)
+    notes[:8, :] = jnp.sum(jnp.where(lane // CTRL_DEV == source, spots, 0.0), axis=1)
     keys = first[:, CTRL_DEV : 2 * CTRL_DEV, :].reshape(CTRL, HEAD_DIM)
     values = first[:, 2 * CTRL_DEV : ROW_M, :].reshape(CTRL, HEAD_DIM)
     for part in range(4):
@@ -88,26 +97,11 @@
         ).astype(BF16)
 
 
-def place_kernel(places, table, first, hint, added, gates):
-    for f in range(FRAMES):
-        gates[f : f + 1, :] = table[pl.ds(places[1 + f], 1), :]
-    meta = first[:, ROW_M:, :].astype(F32)
-    spots = (meta[:, 1, :] * 64.0 + meta[:, 2, :]).reshape(8, 4, 128)
-    source = lax.broadcasted_iota(jnp.int32, (8, 4, 128), 1)
-    lane = lax.broadcasted_iota(jnp.int32, (8, 4, 128), 2)
-    match = jnp.sum(jnp.where(lane // CTRL_DEV == source, spots, 0.0), axis=1)
-    for i in range(SEQ // QB):
-        spot = (lax.broadcasted_iota(jnp.int32, (QB, 128), 0) + i * QB).astype(F32)
-        picks = jnp.concatenate(
-            [jnp.where(spot == match[g : g + 1, :], 1.0, 0.0).astype(BF16) for g in range(8)], axis=1
-        )
-        rows = jnp.dot(picks, hint[...], preferred_element_type=F32).astype(BF16)
-        added[i * (QB // TOK_DEV) : (i + 1) * (QB // TOK_DEV), :, :] = rows.reshape(
-            QB // TOK_DEV, TOK_DEV, HEAD_DIM
-        )
-
-
-def main_kernel(ends_ref, gates, second, added, out, v_t, acc, sums, top_ref):
+def main_kernel(
+    ends_ref, second, hint, notes_hbm, out, notes, match, gates, v_t, hint_t, acc, sums, top_ref, sem
+):
+    copy = pltpu.make_async_copy(notes_hbm, notes, sem)
+    copy.start()
     ends = [ends_ref[f] for f in range(FRAMES)]
 
     def end_of(token):
@@ -121,6 +115,15 @@
             second[block, 2 * TOK_DEV :, :].astype(F32).T.astype(BF16)
         )
     v_t[HEAD_DIM:, :] = jnp.ones((VR - HEAD_DIM, SEQ), BF16)
+    for g in range(CTRL // 128):
+        hint_t[:, g * 128 : g * 128 + 128] = (
+            hint[g * 128 : g * 128 + 128, :].astype(F32).T.astype(BF16)
+        )
+
+    copy.wait()
+    for g in range(8):
+        match[g * 128 : g * 128 + 128, :] = jnp.broadcast_to(notes[g : g + 1, :], (128, 128)).T
+        gates[g, :, :] = jnp.broadcast_to(notes[8 + g : 9 + g, :], (128, 128)).T
 
     def limit_of(base):
         column = lax.broadcasted_iota(jnp.int32, (8, QB), 1) + base
@@ -144,42 +147,52 @@
 
     def finish(i, total):
         base = i * QB
-        token = lax.broadcasted_iota(jnp.int32, (QB, HEAD_DIM), 0) + base
-        attn = (total[:HEAD_DIM, :] / total[HEAD_DIM : HEAD_DIM + 1, :]).T.astype(BF16).astype(F32)
-        gate = jnp.broadcast_to(gates[0:1, :], (QB, HEAD_DIM))
-        for f in range(1, FRAMES):
-            gate = jnp.where(token >= ends[f - 1], gates[f : f + 1, :], gate)
-        at = pl.ds(i * (QB // TOK_DEV), QB // TOK_DEV)
-        rows = added[at, :, :].reshape(QB, HEAD_DIM).astype(F32)
-        out[at, :, :] = (gate * attn + rows).astype(BF16).reshape(QB // TOK_DEV, TOK_DEV, HEAD_DIM)
+        attn = (total[:HEAD_DIM, :] / total[HEAD_DIM : HEAD_DIM + 1, :]).astype(BF16).astype(F32)
+        picks, gate = [], []
+        for at in range(0, QB, 128):
+            spot = lax.broadcasted_iota(jnp.int32, (CTRL, 128), 1).astype(F32)
+            shift = jnp.asarray(base + at, F32)
+            picks.append(jnp.where(match[...] - shift == spot, 1.0, 0.0).astype(BF16))
+            token = lax.broadcasted_iota(jnp.int32, (HEAD_DIM, 128), 1) + base + at
+            level = gates[0]
+            for f in range(1, FRAMES):
+                level = jnp.where(token >= ends[f - 1], gates[f], level)
+            gate.append(level)
+        added = jnp.dot(hint_t[...], jnp.concatenate(picks, axis=1), preferred_element_type=F32)
+        mixed = (jnp.concatenate(gate, axis=1) * attn + added).T.astype(BF16)
+        rows = QB // TOK_DEV
+        out[pl.ds(i * rows, rows), :, :] = mixed.reshape(rows, TOK_DEV, HEAD_DIM)
 
     def quick_block(i, carry):
         base = i * QB
-        n_full = end_of(base) // KB
-        n_all = (end_of(base + QB - 1) + KB - 1) // KB
         limit = limit_of(base)
         queries = second[pl.ds(i * (QB // TOK_DEV), QB // TOK_DEV), :TOK_DEV, :]
         q_t = queries.reshape(QB, HEAD_DIM).astype(F32).T.astype(BF16)
-        acc[...] = jnp.zeros_like(acc)
-
-        def step(j, masked):
-            keys = second[pl.ds(j * (KB // TOK_DEV), KB // TOK_DEV), TOK_DEV : 2 * TOK_DEV, :]
-            scores = jnp.dot(keys.reshape(KB, HEAD_DIM), q_t, preferred_element_type=F32)
-            expo = jnp.exp2(scores * SCALE2)
-            if masked:
-                expo = jnp.where(visible(limit, j), expo, 0.0)
-            acc[...] += jnp.dot(values_of(j), expo.astype(BF16), preferred_element_type=F32)
-
-        @pl.loop(0, n_full)
-        def _(j):
-            step(j, False)
-
-        @pl.loop(n_full, n_all)
-        def _(j):
-            step(j, True)
+
+        def run(count):
+            finish(jnp.maximum(i - 1, 0), acc)
+            total = None
+            edge = max(0, count - 3)
+            cuts = list(range(0, edge, WIDE)) + list(range(edge, count)) + [count]
+            for c, d in zip(cuts[:-1], cuts[1:]):
+                per = PART // TOK_DEV
+                keys = second[c * per : d * per, TOK_DEV : 2 * TOK_DEV, :]
+                keys = keys.reshape((d - c) * PART, HEAD_DIM)
+                expo = jnp.exp2(jnp.dot(keys, q_t, preferred_element_type=F32) * SCALE2)
+                if c >= edge:
+                    row = lax.broadcasted_iota(jnp.int32, expo.shape, 0)
+                    expo = jnp.where(row < limit - c * PART, expo, 0.0)
+                part = jnp.dot(
+                    v_t[:, c * PART : d * PART], expo.astype(BF16), preferred_element_type=F32
+                )
+                total = part if total is None else total + part
+            acc[...] = total
+
+        parts = (end_of(base + QB - 1) + PART - 1) // PART
+        for count in range(1, SEQ // PART + 1):
+            pl.when(parts == count)(functools.partial(run, count))
 
         sums[pl.ds(i, 1), :] = acc[HEAD_DIM : HEAD_DIM + 1, :]
-        finish(i, acc)
         return carry
 
     def full_block(i, carry):
@@ -202,7 +215,9 @@
         finish(i, acc)
         return carry
 
+    acc[...] = jnp.ones_like(acc)
     lax.fori_loop(0, SEQ // QB, quick_block, 0)
+    finish(SEQ // QB - 1, acc)
     good = (sums[...] > 1.0 / SAFE) & (sums[...] < SAFE)
     count = jnp.sum(jnp.where(good, 1.0, 0.0))
 
@@ -224,22 +239,27 @@
     return jax.ShapeDtypeStruct(dims, dtype)
 
 
-def run_main(ends, gates, second, added):
+def run_main(ends, second, hint, notes):
     return pl.pallas_call(
         main_kernel,
         out_shape=shape(HEADS, TOK_DEV, HEAD_DIM),
-        in_specs=[pl.BlockSpec(memory_space=pltpu.SMEM), whole(), whole(), whole()],
+        in_specs=[pl.BlockSpec(memory_space=pltpu.SMEM)] + [whole()] * 2 + [pl.BlockSpec(memory_space=pltpu.HBM)],
         out_specs=whole(),
         scratch_shapes=[
+            pltpu.VMEM((16, 128), F32),
+            pltpu.VMEM((CTRL, 128), F32),
+            pltpu.VMEM((FRAMES, HEAD_DIM, 128), F32),
             pltpu.VMEM((VR, SEQ), BF16),
+            pltpu.VMEM((HEAD_DIM, CTRL), BF16),
             pltpu.VMEM((VR, QB), F32),
             pltpu.VMEM((SEQ // QB, QB), F32),
             pltpu.VMEM((8, QB), F32),
+            pltpu.SemaphoreType.DMA,
         ],
         compiler_params=params(),
         cost_estimate=cost(4 * SEQ * SEQ * HEAD_DIM, 5_000_000, SEQ * SEQ),
         name="main_attention",
-    )(ends, gates, second, added)
+    )(ends, second, hint, notes)
 
 
 def exchange(block):
@@ -267,7 +287,7 @@
         out_shape=shape(HEADS, ROWS_C, HEAD_DIM),
         in_specs=[whole()] * 7,
         out_specs=whole(),
-        compiler_params=params(),
+        compiler_params=params(56),
         cost_estimate=cost(2_000_000, 2_000_000),
         name="pack_ctrl",
     )(
@@ -290,36 +310,27 @@
         name="pack_main",
     )(query[0], key[0], value[0], gain_query[None], gain_key[None])
     second = exchange(packed_main)
-    hint, ends = pl.pallas_call(
+    places = jnp.concatenate([lax.axis_index("seq")[None].astype(jnp.int32), levels[0]])
+    hint, ends, notes = pl.pallas_call(
         ctrl_kernel,
-        out_shape=(shape(CTRL, HEAD_DIM), shape(FRAMES, dtype=jnp.int32)),
-        in_specs=[whole()],
-        out_specs=(whole(), pl.BlockSpec(memory_space=pltpu.SMEM)),
+        grid_spec=pltpu.PrefetchScalarGridSpec(
+            num_scalar_prefetch=1,
+            grid=(1,),
+            in_specs=[pl.BlockSpec((LEVELS, HEAD_DIM), lambda i, places: (0, places[0])), whole()],
+            out_specs=(whole(), pl.BlockSpec(memory_space=pltpu.SMEM), whole()),
+        ),
+        out_shape=(
+            shape(CTRL, HEAD_DIM),
+            shape(FRAMES, dtype=jnp.int32),
+            shape(16, 128, dtype=F32),
+        ),
         compiler_params=params(),
         cost_estimate=cost(4 * CTRL * CTRL * HEAD_DIM, 1_000_000, CTRL * CTRL),
         name="ctrl_attention",
-    )(first)
+    )(places, gate_table, first)
     groups = lax.axis_size("grp")
     hint = lax.ppermute(hint, "grp", [((i - 1) % groups, i) for i in range(groups)])
-    places = jnp.concatenate([lax.axis_index("seq")[None].astype(jnp.int32), levels[0]])
-    added, gates = pl.pallas_call(
-        place_kernel,
-        grid_spec=pltpu.PrefetchScalarGridSpec(
-            num_scalar_prefetch=1,
-            grid=(1,),
-            in_specs=[
-                pl.BlockSpec((LEVELS, HEAD_DIM), lambda i, places: (0, places[0])),
-                whole(),
-                whole(),
-            ],
-            out_specs=(whole(), whole()),
-        ),
-        out_shape=(shape(HEADS, TOK_DEV, HEAD_DIM), shape(FRAMES, HEAD_DIM, dtype=F32)),
-        compiler_params=params(),
-        cost_estimate=cost(2 * SEQ * CTRL * HEAD_DIM, 2_000_000),
-        name="place_hints",
-    )(places, gate_table, first, hint)
-    mixed = run_main(ends, gates, second, added)
+    mixed = run_main(ends, second, hint, notes)
     back = exchange(mixed)
     return pl.pallas_call(
         unpack_kernel,

time: 152 us -> 142 us (0.934); the launches traced: 152 us -> 139 us
  local copies, waits for them, and re-layouts: 7.95 us -> 0.03 us
  Pallas kernels: 33.8 us -> 29.9 us
  blocking collectives: 53.2 us -> 50.8 us
    unnamed x32 -> x14, local copies, waits for them, and re-layouts: 7.95 us -> 0.03 us
    pallas_call x2 -> x1, Pallas kernels: 8.6 us -> 5.05 us  [body(): pl.pallas_call(ctrl_kernel, grid_spec=pltpu.PrefetchScalarGridSpec(num_sc...]
    all_to_all x1, blocking collectives: 53.2 us -> 50.8 us  [exchange(): return lax.all_to_all(block, 'seq', split_axis=0, concat_axis=0, tiled=True)]
    all_to_all x2, waiting for transfers between devices: 12.4 us -> 14.3 us  [exchange(): return lax.all_to_all(block, 'seq', split_axis=0, concat_axis=0, tiled=True)]
    pallas_call x1, Pallas kernels: 19.8 us -> 18.1 us  [run_main(): pl.pallas_call(main_kernel, out_shape=shape(HEADS, TOK_DEV, HEAD_DIM), in...]
  transfers between devices with their start and end apart: 3 -> 3, of which waited for: 2 -> 3; matrix products, arithmetic and copies ran while one was open for 0% -> 0% of each run, Pallas kernels for 8% -> 6%
where the time goes in v3:
time: 142 us; the launch traced here: 139 us
  blocking collectives  50.8 us (36%)
  waiting for transfers between devices  45.5 us (32%)
  Pallas kernels  29.9 us (21%)
  starting transfers between devices  12.9 us (9%)
    all_to_all x1, blocking collectives, exchange(): return lax.all_to_all(block, 'seq', split_axis=0, concat_axis=0, tiled=True)  50.8 us
    ppermute x1, waiting for transfers between devices, body(): lax.ppermute(hint, 'grp', [((i - 1) % groups, i) for i in range(groups)])  31.2 us
    pallas_call x1, Pallas kernels, run_main(): pl.pallas_call(main_kernel, out_shape=shape(HEADS, TOK_DEV, HEAD_DIM), in...  18.1 us
    all_to_all x2, waiting for transfers between devices, exchange(): return lax.all_to_all(block, 'seq', split_axis=0, concat_axis=0, tiled=True)  14.3 us
    all_to_all x2, starting transfers between devices, exchange(): return lax.all_to_all(block, 'seq', split_axis=0, concat_axis=0, tiled=True)  12.8 us
    pallas_call x1, Pallas kernels, body(): pl.pallas_call(ctrl_kernel, grid_spec=pltpu.PrefetchScalarGridSpec(num_sc...  5.05 us
    pallas_call x1, Pallas kernels, body(): pl.pallas_call(pack_main_kernel, out_shape=shape(HEADS, ROWS, HEAD_DIM),...  2.94 us
  transfers between devices with their start and end apart: 3, of which 3 were waited for; matrix products, arithmetic and copies ran while one was open for 0% of the time, Pallas kernels for 6%

profile of v3, /device:TPU:64, one launch (start us, length us, event | category | flops | bytes accessed | tf_op | source)
XLA Modules:
  0.0 139.4 jit_solution(9323525920893669045)
XLA Ops:
  0.0 0.0 copy-start.4
  0.0 0.0 copy-start.3
  0.0 0.0 copy-start.2
  0.0 0.0 copy-start.1
  0.0 0.0 copy-start
  0.0 2.5 %pack_ctrl.1 = bf16[32,112,128]{2,1,0:T(8,128)(2,1)} custom-call(bf16[32,4096]{1,0:T(8,128)(2,1)} %bitcast.18, bf16[32,4096]{1,0:T(8,128)(2,1)} %bitcast.19, bf16[32,4096]{1,0:T(8,128)(2,1)} %bitcast.20, f32[1,4096]{1,0:T(1,128)} %bitcast.21, f32[1,4096]{1,0:T(1,128)} %bitcast.22, s32[1,128]{1,0:T(1,128)} %frames.1, s32[1,32]{1,0:T(1,128)} %match.1), custom_call_target="tpu_custom_call" | custom-call | flops 2000000 | bytes 2000000 | tf_op jit(solution)/shard_map/pack_ctrl/pallas_call | solution.py:285
  2.6 8.5 %all-to-all-start = ((bf16[32,112,128]{2,1,0:T(8,128)(2,1)}), bf16[32,112,128]{2,1,0:T(8,128)(2,1)}, u32[]{:S(2)}, u32[]{:S(2)}) async-start(bf16[32,112,128]{2,1,0:T(8,128)(2,1)} %pack_ctrl.1), calls=%async_computation | async-start | bytes 1835008 | tf_op jit(solution)/shard_map/all_to_all | solution.py:266
  11.1 0.0 copy-done.4
  11.1 0.0 copy-done.3
  11.1 0.0 copy-done.2
  11.1 0.0 copy-done.1
  11.1 0.0 copy-done
  11.1 2.9 %pack_main.1 = bf16[32,384,128]{2,1,0:T(8,128)(2,1)} custom-call(bf16[128,4096]{1,0:T(8,128)(2,1)S(1)} %bitcast.13, bf16[128,4096]{1,0:T(8,128)(2,1)S(1)} %bitcast.14, bf16[128,4096]{1,0:T(8,128)(2,1)S(1)} %bitcast.15, f32[1,4096]{1,0:T(1,128)S(1)} %bitcast.16, f32[1,4096]{1,0:T(1,128)S(1)} %bitcast.17), custom_call_target="tpu_custom_call" | custom-call | flops 8000000 | bytes 6000000 | tf_op jit(solution)/shard_map/pack_main/pallas_call | solution.py:303
  14.1 0.0 copy-start.6
  14.1 0.0 copy-start.5
  14.1 12.4 %all-to-all-done.first = bf16[32,112,128]{2,1,0:T(8,128)(2,1)} async-done(((bf16[32,112,128]{2,1,0:T(8,128)(2,1)}), bf16[32,112,128]{2,1,0:T(8,128)(2,1)}, u32[]{:S(2)}, u32[]{:S(2)}) %all-to-all-start) | async-done | bytes 917536 | tf_op jit(solution)/shard_map/all_to_all | solution.py:266
  26.5 4.3 %all-to-all-start.1 = ((bf16[32,384,128]{2,1,0:T(8,128)(2,1)}), bf16[32,384,128]{2,1,0:T(8,128)(2,1)S(1)}, u32[]{:S(2)}, u32[]{:S(2)}) async-start(bf16[32,384,128]{2,1,0:T(8,128)(2,1)} %pack_main.1), calls=%async_computation.1 | async-start | bytes 6291456 | tf_op jit(solution)/shard_map/all_to_all | solution.py:266
  30.9 0.0 copy-done.6
  30.9 0.1 pad_add_fusion.places
  31.0 0.0 copy-done.5
  31.0 5.0 %ctrl_attention.1 = (bf16[1024,128]{1,0:T(8,128)(2,1)S(1)}, s32[8]{0:T(128)S(1)}, f32[16,128]{1,0:T(8,128)S(1)}) custom-call(s32[9]{0:T(128)S(1)} %pad_add_fusion.places, f32[16,4096]{1,0:T(8,128)S(1)} %copy-done.5, bf16[32,112,128]{2,1,0:T(8,128)(2,1)} %all-to-all-done.first), custom_call_target="tpu_custom_call" | custom-call | flops 536870912 | bytes 1000000 | tf_op jit(solution)/shard_map/ctrl_attention/pallas_call | solution.py:314
  36.0 0.1 collective-permute-start
  36.1 31.2 %collective-permute-done.hint = bf16[1024,128]{1,0:T(8,128)(2,1)S(1)} collective-permute-done((bf16[1024,128]{1,0:T(8,128)(2,1)S(1)}, bf16[1024,128]{1,0:T(8,128)(2,1)S(1)}, u32[]{:S(2)}, u32[]{:S(2)}) %collective-permute-start) | collective-permute-done | bytes 262176 | tf_op jit(solution)/shard_map/ppermute | solution.py:332
  67.3 1.9 %all-to-all-done.1.second = bf16[32,384,128]{2,1,0:T(8,128)(2,1)S(1)} async-done(((bf16[32,384,128]{2,1,0:T(8,128)(2,1)}), bf16[32,384,128]{2,1,0:T(8,128)(2,1)S(1)}, u32[]{:S(2)}, u32[]{:S(2)}) %all-to-all-start.1) | async-done | bytes 3145760 | tf_op jit(solution)/shard_map/all_to_all | solution.py:266
  69.2 18.1 %main_attention.1 = bf16[32,128,128]{2,1,0:T(8,128)(2,1)S(1)} custom-call(s32[8]{0:T(128)S(1)} %get-tuple-element.8.ends_ref, bf16[32,384,128]{2,1,0:T(8,128)(2,1)S(1)} %all-to-all-done.1.second, bf16[1024,128]{1,0:T(8,128)(2,1)S(1)} %collective-permute-done.hint, f32[16,128]{1,0:T(8,128)S(1)} %get-tuple-element.10.notes_hbm), custom_call_target="tpu_custom_call" | custom-call | flops 8589934592 | bytes 5000000 | tf_op jit(solution)/shard_map/main_attention/pallas_call | solution.py:243
  87.3 50.8 %all_to_all.15.rows = bf16[32,128,128]{2,1,0:T(8,128)(2,1)S(1)} all-to-all(bf16[32,128,128]{2,1,0:T(8,128)(2,1)S(1)} %main_attention.1), channel_id=1, replica_groups=mesh['grp'=4,'seq'=32] {'seq'}, dimensions={0} | all-to-all | bytes 2097152 | tf_op jit(solution)/shard_map/all_to_all | solution.py:266
  138.1 1.2 unpack.1
Async XLA Ops:
  0.0 11.1 %copy-start.4 = (f32[4096]{0:T(1024)S(1)}, f32[4096]{0:T(1024)}, u32[]{:S(2)}) copy-start(f32[4096]{0:T(1024)} %param.18) | copy-start | bytes 49156
  0.0 11.1 %copy-start.3 = (f32[4096]{0:T(1024)S(1)}, f32[4096]{0:T(1024)}, u32[]{:S(2)}) copy-start(f32[4096]{0:T(1024)} %param.17) | copy-start | bytes 49156
  0.0 11.1 %copy-start.2 = (bf16[1,128,4096]{2,1,0:T(8,128)(2,1)S(1)}, bf16[1,128,4096]{2,1,0:T(8,128)(2,1)}, u32[]{:S(2)}) copy-start(bf16[1,128,4096]{2,1,0:T(8,128)(2,1)} %param.16) | copy-start | bytes 3145732
  0.0 11.1 %copy-start.1 = (bf16[1,128,4096]{2,1,0:T(8,128)(2,1)S(1)}, bf16[1,128,4096]{2,1,0:T(8,128)(2,1)}, u32[]{:S(2)}) copy-start(bf16[1,128,4096]{2,1,0:T(8,128)(2,1)} %param.15) | copy-start | bytes 3145732
  0.0 11.1 %copy-start = (bf16[1,128,4096]{2,1,0:T(8,128)(2,1)S(1)}, bf16[1,128,4096]{2,1,0:T(8,128)(2,1)}, u32[]{:S(2)}) copy-start(bf16[1,128,4096]{2,1,0:T(8,128)(2,1)} %param.14) | copy-start | bytes 3145732
  2.6 23.9 %all-to-all-start = ((bf16[32,112,128]{2,1,0:T(8,128)(2,1)}), bf16[32,112,128]{2,1,0:T(8,128)(2,1)}, u32[]{:S(2)}, u32[]{:S(2)}) async-start(bf16[32,112,128]{2,1,0:T(8,128)(2,1)} %pack_ctrl.1), calls=%async_computation | async-start | bytes 1835008 | tf_op jit(solution)/shard_map/all_to_all | solution.py:266
  14.1 16.8 %copy-start.6 = (s32[1,8]{1,0:T(1,128)S(1)}, s32[1,8]{1,0:T(1,128)}, u32[]{:S(2)}) copy-start(s32[1,8]{1,0:T(1,128)} %param.25) | copy-start | bytes 100
  14.1 16.9 %copy-start.5 = (f32[16,4096]{1,0:T(8,128)S(1)}, f32[16,4096]{1,0:T(8,128)}, u32[]{:S(2)}) copy-start(f32[16,4096]{1,0:T(8,128)} %table.1) | copy-start | bytes 786436
  26.5 42.7 %all-to-all-start.1 = ((bf16[32,384,128]{2,1,0:T(8,128)(2,1)}), bf16[32,384,128]{2,1,0:T(8,128)(2,1)S(1)}, u32[]{:S(2)}, u32[]{:S(2)}) async-start(bf16[32,384,128]{2,1,0:T(8,128)(2,1)} %pack_main.1), calls=%async_computation.1 | async-start | bytes 6291456 | tf_op jit(solution)/shard_map/all_to_all | solution.py:266
  36.0 31.3 %collective-permute-start = (bf16[1024,128]{1,0:T(8,128)(2,1)S(1)}, bf16[1024,128]{1,0:T(8,128)(2,1)S(1)}, u32[]{:S(2)}, u32[]{:S(2)}) collective-permute-start(bf16[1024,128]{1,0:T(8,128)(2,1)S(1)} %get-tuple-element.9), channel_id=1, source_target_pairs={{96,0},{0,32},{32,64},{64,96},{97,1},{1,33},{33,65},{65,97},{98,2}... | collective-permute-start | bytes 786440 | tf_op jit(solution)/shard_map/ppermute | solution.py:332

commit v4 on v3

--- a/solution.py
+++ b/solution.py
@@ -24,7 +24,7 @@
 SCALE2 = math.log2(math.e) / math.sqrt(HEAD_DIM)
 QB = 512
 KB = 1024
-PART = 512
+PART = 256
 WIDE = 8
 VR = HEAD_DIM + 16
 SAFE = 2.0**100
@@ -65,12 +65,19 @@
         out[head, ROW_M:, :] = meta
 
 
-def pack_main_kernel(q, k, v, gq, gk, out):
+def turned(block):
+    return block.astype(F32).T.astype(BF16)
+
+
+def pack_main_kernel(q, k, v, gq, gk, out, q_norm):
     step = 32
     for at in range(0, TOK_DEV, step):
-        lay_heads(out, at, rms_round(q[at : at + step, :], gq[...]))
+        q_norm[at : at + step, :] = rms_round(q[at : at + step, :], gq[...])
         lay_heads(out, TOK_DEV + at, rms_round(k[at : at + step, :], gk[...]))
-        lay_heads(out, 2 * TOK_DEV + at, v[at : at + step, :])
+    for head in range(HEADS):
+        lanes = slice(head * HEAD_DIM, (head + 1) * HEAD_DIM)
+        out[head, :TOK_DEV, :] = turned(q_norm[:, lanes])
+        out[head, 2 * TOK_DEV :, :] = turned(v[:, lanes])
 
 
 def ctrl_kernel(places, table, first, hint, ends, notes):
@@ -92,13 +99,12 @@
         expo = jnp.exp2((scores - top) * SCALE2)
         total = jnp.sum(expo, axis=1, keepdims=True)
         weights = (expo * (1.0 / total)).astype(BF16)
-        hint[part * 256 : part * 256 + 256, :] = jnp.dot(
-            weights, values, preferred_element_type=F32
-        ).astype(BF16)
+        rows = jnp.dot(weights, values, preferred_element_type=F32).astype(BF16)
+        hint[:, part * 256 : part * 256 + 256] = turned(rows)
 
 
 def main_kernel(
-    ends_ref, second, hint, notes_hbm, out, notes, match, gates, v_t, hint_t, acc, sums, top_ref, sem
+    ends_ref, second, hint, notes_hbm, out, notes, match, gates, v_t, acc, sums, top_ref, sem
 ):
     copy = pltpu.make_async_copy(notes_hbm, notes, sem)
     copy.start()
@@ -111,15 +117,8 @@
         return end
 
     for block in range(HEADS):
-        v_t[:HEAD_DIM, block * 128 : block * 128 + 128] = (
-            second[block, 2 * TOK_DEV :, :].astype(F32).T.astype(BF16)
-        )
+        v_t[:HEAD_DIM, block * 128 : block * 128 + 128] = second[block, 2 * TOK_DEV :, :]
     v_t[HEAD_DIM:, :] = jnp.ones((VR - HEAD_DIM, SEQ), BF16)
-    for g in range(CTRL // 128):
-        hint_t[:, g * 128 : g * 128 + 128] = (
-            hint[g * 128 : g * 128 + 128, :].astype(F32).T.astype(BF16)
-        )
-
     copy.wait()
     for g in range(8):
         match[g * 128 : g * 128 + 128, :] = jnp.broadcast_to(notes[g : g + 1, :], (128, 128)).T
@@ -132,9 +131,12 @@
             limit = jnp.where(ends[f] > column, ends[f], limit)
         return limit[:1, :]
 
+    def queries_of(i):
+        per = QB // TOK_DEV
+        return jnp.concatenate([second[i * per + n, :TOK_DEV, :] for n in range(per)], axis=1)
+
     def scores_of(i, j, masked):
-        queries = second[pl.ds(i * (QB // TOK_DEV), QB // TOK_DEV), :TOK_DEV, :]
-        q_t = queries.reshape(QB, HEAD_DIM).astype(F32).T.astype(BF16)
+        q_t = queries_of(i)
         keys = second[pl.ds(j * (KB // TOK_DEV), KB // TOK_DEV), TOK_DEV : 2 * TOK_DEV, :]
         scores = jnp.dot(keys.reshape(KB, HEAD_DIM), q_t, preferred_element_type=F32)
         return scores
@@ -147,18 +149,17 @@
 
     def finish(i, total):
         base = i * QB
-        attn = (total[:HEAD_DIM, :] / total[HEAD_DIM : HEAD_DIM + 1, :]).astype(BF16).astype(F32)
+        attn = (total[:HEAD_DIM, :] * (1.0 / total[HEAD_DIM : HEAD_DIM + 1, :])).astype(BF16).astype(F32)
         picks, gate = [], []
         for at in range(0, QB, 128):
-            spot = lax.broadcasted_iota(jnp.int32, (CTRL, 128), 1).astype(F32)
-            shift = jnp.asarray(base + at, F32)
-            picks.append(jnp.where(match[...] - shift == spot, 1.0, 0.0).astype(BF16))
+            spot = (lax.broadcasted_iota(jnp.int32, (1, 128), 1) + (base + at)).astype(F32)
+            picks.append(jnp.where(match[...] == spot, 1.0, 0.0).astype(BF16))
             token = lax.broadcasted_iota(jnp.int32, (HEAD_DIM, 128), 1) + base + at
             level = gates[0]
             for f in range(1, FRAMES):
                 level = jnp.where(token >= ends[f - 1], gates[f], level)
             gate.append(level)
-        added = jnp.dot(hint_t[...], jnp.concatenate(picks, axis=1), preferred_element_type=F32)
+        added = jnp.dot(hint[...], jnp.concatenate(picks, axis=1), preferred_element_type=F32)
         mixed = (jnp.concatenate(gate, axis=1) * attn + added).T.astype(BF16)
         rows = QB // TOK_DEV
         out[pl.ds(i * rows, rows), :, :] = mixed.reshape(rows, TOK_DEV, HEAD_DIM)
@@ -166,14 +167,13 @@
     def quick_block(i, carry):
         base = i * QB
         limit = limit_of(base)
-        queries = second[pl.ds(i * (QB // TOK_DEV), QB // TOK_DEV), :TOK_DEV, :]
-        q_t = queries.reshape(QB, HEAD_DIM).astype(F32).T.astype(BF16)
+        q_t = queries_of(i)
 
         def run(count):
             finish(jnp.maximum(i - 1, 0), acc)
             total = None
-            edge = max(0, count - 3)
-            cuts = list(range(0, edge, WIDE)) + list(range(edge, count)) + [count]
+            edge = max(0, count - 3 * QB // PART)
+            cuts = sorted({0, edge}) + [count]
             for c, d in zip(cuts[:-1], cuts[1:]):
                 per = PART // TOK_DEV
                 keys = second[c * per : d * per, TOK_DEV : 2 * TOK_DEV, :]
@@ -250,7 +250,6 @@
             pltpu.VMEM((CTRL, 128), F32),
             pltpu.VMEM((FRAMES, HEAD_DIM, 128), F32),
             pltpu.VMEM((VR, SEQ), BF16),
-            pltpu.VMEM((HEAD_DIM, CTRL), BF16),
             pltpu.VMEM((VR, QB), F32),
             pltpu.VMEM((SEQ // QB, QB), F32),
             pltpu.VMEM((8, QB), F32),
@@ -305,6 +304,7 @@
         out_shape=shape(HEADS, ROWS, HEAD_DIM),
         in_specs=[whole()] * 5,
         out_specs=whole(),
+        scratch_shapes=[pltpu.VMEM((TOK_DEV, WIDTH), BF16)],
         compiler_params=params(),
         cost_estimate=cost(8_000_000, 6_000_000),
         name="pack_main",
@@ -320,7 +320,7 @@
             out_specs=(whole(), pl.BlockSpec(memory_space=pltpu.SMEM), whole()),
         ),
         out_shape=(
-            shape(CTRL, HEAD_DIM),
+            shape(HEAD_DIM, CTRL),
             shape(FRAMES, dtype=jnp.int32),
             shape(16, 128, dtype=F32),
         ),

time: 142 us -> 137 us (0.965); the launches traced: 139 us -> 137 us
  blocking collectives: 50.8 us -> 49.2 us
    all_to_all x1, blocking collectives: 50.8 us -> 49.2 us  [exchange(): return lax.all_to_all(block, 'seq', split_axis=0, concat_axis=0, tiled=True)]
where the time goes in v4:
time: 137 us
  blocking collectives  49.2 us (36%)
  waiting for transfers between devices  45.3 us (33%)
  Pallas kernels  29.5 us (22%)
  starting transfers between devices  12.9 us (9%)
    all_to_all x1, blocking collectives, exchange(): return lax.all_to_all(block, 'seq', split_axis=0, concat_axis=0, tiled=True)  49.2 us
    ppermute x1, waiting for transfers between devices, body(): lax.ppermute(hint, 'grp', [((i - 1) % groups, i) for i in range(groups)])  31.3 us
    pallas_call x1, Pallas kernels, run_main(): pl.pallas_call(main_kernel, out_shape=shape(HEADS, TOK_DEV, HEAD_DIM), in...  17.5 us
    all_to_all x2, waiting for transfers between devices, exchange(): return lax.all_to_all(block, 'seq', split_axis=0, concat_axis=0, tiled=True)  14 us
    all_to_all x2, starting transfers between devices, exchange(): return lax.all_to_all(block, 'seq', split_axis=0, concat_axis=0, tiled=True)  12.8 us
    pallas_call x1, Pallas kernels, body(): pl.pallas_call(ctrl_kernel, grid_spec=pltpu.PrefetchScalarGridSpec(num_sc...  4.97 us
    pallas_call x1, Pallas kernels, body(): pl.pallas_call(pack_main_kernel, out_shape=shape(HEADS, ROWS, HEAD_DIM),...  3.26 us
  transfers between devices with their start and end apart: 3, of which 3 were waited for; matrix products, arithmetic and copies ran while one was open for 0% of the time, Pallas kernels for 6%

profile of v4, /device:TPU:64, one launch (start us, length us, event | category | flops | bytes accessed | tf_op | source)
XLA Modules:
  0.0 137.2 jit_solution(10644757457136135314)
XLA Ops:
  0.0 0.0 copy-start.4
  0.0 0.0 copy-start.3
  0.0 0.0 copy-start.2
  0.0 0.0 copy-start.1
  0.0 0.0 copy-start
  0.0 2.5 %pack_ctrl.1 = bf16[32,112,128]{2,1,0:T(8,128)(2,1)} custom-call(bf16[32,4096]{1,0:T(8,128)(2,1)} %bitcast.18, bf16[32,4096]{1,0:T(8,128)(2,1)} %bitcast.19, bf16[32,4096]{1,0:T(8,128)(2,1)} %bitcast.20, f32[1,4096]{1,0:T(1,128)} %bitcast.21, f32[1,4096]{1,0:T(1,128)} %bitcast.22, s32[1,128]{1,0:T(1,128)} %frames.1, s32[1,32]{1,0:T(1,128)} %match.1), custom_call_target="tpu_custom_call" | custom-call | flops 2000000 | bytes 2000000 | tf_op jit(solution)/shard_map/pack_ctrl/pallas_call | solution.py:284
  2.6 8.5 %all-to-all-start = ((bf16[32,112,128]{2,1,0:T(8,128)(2,1)}), bf16[32,112,128]{2,1,0:T(8,128)(2,1)}, u32[]{:S(2)}, u32[]{:S(2)}) async-start(bf16[32,112,128]{2,1,0:T(8,128)(2,1)} %pack_ctrl.1), calls=%async_computation | async-start | bytes 1835008 | tf_op jit(solution)/shard_map/all_to_all | solution.py:265
  11.1 0.0 copy-done.4
  11.1 0.0 copy-done.3
  11.1 0.0 copy-done.2
  11.1 0.0 copy-done.1
  11.1 0.0 copy-done
  11.1 3.3 %pack_main.1 = bf16[32,384,128]{2,1,0:T(8,128)(2,1)} custom-call(bf16[128,4096]{1,0:T(8,128)(2,1)S(1)} %bitcast.13, bf16[128,4096]{1,0:T(8,128)(2,1)S(1)} %bitcast.14, bf16[128,4096]{1,0:T(8,128)(2,1)S(1)} %bitcast.15, f32[1,4096]{1,0:T(1,128)S(1)} %bitcast.16, f32[1,4096]{1,0:T(1,128)S(1)} %bitcast.17), custom_call_target="tpu_custom_call" | custom-call | flops 8000000 | bytes 6000000 | tf_op jit(solution)/shard_map/pack_main/pallas_call | solution.py:302
  14.4 0.0 copy-start.6
  14.4 0.0 copy-start.5
  14.4 12.1 %all-to-all-done.first = bf16[32,112,128]{2,1,0:T(8,128)(2,1)} async-done(((bf16[32,112,128]{2,1,0:T(8,128)(2,1)}), bf16[32,112,128]{2,1,0:T(8,128)(2,1)}, u32[]{:S(2)}, u32[]{:S(2)}) %all-to-all-start) | async-done | bytes 917536 | tf_op jit(solution)/shard_map/all_to_all | solution.py:265
  26.5 4.3 %all-to-all-start.1 = ((bf16[32,384,128]{2,1,0:T(8,128)(2,1)}), bf16[32,384,128]{2,1,0:T(8,128)(2,1)S(1)}, u32[]{:S(2)}, u32[]{:S(2)}) async-start(bf16[32,384,128]{2,1,0:T(8,128)(2,1)} %pack_main.1), calls=%async_computation.1 | async-start | bytes 6291456 | tf_op jit(solution)/shard_map/all_to_all | solution.py:265
  30.9 0.0 copy-done.6
  30.9 0.1 pad_add_fusion.places
  31.0 0.0 copy-done.5
  31.0 5.0 %ctrl_attention.1 = (bf16[128,1024]{1,0:T(8,128)(2,1)S(1)}, s32[8]{0:T(128)S(1)}, f32[16,128]{1,0:T(8,128)S(1)}) custom-call(s32[9]{0:T(128)S(1)} %pad_add_fusion.places, f32[16,4096]{1,0:T(8,128)S(1)} %copy-done.5, bf16[32,112,128]{2,1,0:T(8,128)(2,1)} %all-to-all-done.first), custom_call_target="tpu_custom_call" | custom-call | flops 536870912 | bytes 1000000 | tf_op jit(solution)/shard_map/ctrl_attention/pallas_call | solution.py:314
  36.0 0.1 collective-permute-start
  36.0 31.3 %collective-permute-done.hint = bf16[128,1024]{1,0:T(8,128)(2,1)S(1)} collective-permute-done((bf16[128,1024]{1,0:T(8,128)(2,1)S(1)}, bf16[128,1024]{1,0:T(8,128)(2,1)S(1)}, u32[]{:S(2)}, u32[]{:S(2)}) %collective-permute-start) | collective-permute-done | bytes 262176 | tf_op jit(solution)/shard_map/ppermute | solution.py:332
  67.3 1.9 %all-to-all-done.1.second = bf16[32,384,128]{2,1,0:T(8,128)(2,1)S(1)} async-done(((bf16[32,384,128]{2,1,0:T(8,128)(2,1)}), bf16[32,384,128]{2,1,0:T(8,128)(2,1)S(1)}, u32[]{:S(2)}, u32[]{:S(2)}) %all-to-all-start.1) | async-done | bytes 3145760 | tf_op jit(solution)/shard_map/all_to_all | solution.py:265
  69.2 17.5 %main_attention.1 = bf16[32,128,128]{2,1,0:T(8,128)(2,1)S(1)} custom-call(s32[8]{0:T(128)S(1)} %get-tuple-element.8.ends_ref, bf16[32,384,128]{2,1,0:T(8,128)(2,1)S(1)} %all-to-all-done.1.second, bf16[128,1024]{1,0:T(8,128)(2,1)S(1)} %collective-permute-done.hint, f32[16,128]{1,0:T(8,128)S(1)} %get-tuple-element.10.notes_hbm), custom_call_target="tpu_custom_call" | custom-call | flops 8589934592 | bytes 5000000 | tf_op jit(solution)/shard_map/main_attention/pallas_call | solution.py:243
  86.7 49.2 %all_to_all.15.rows = bf16[32,128,128]{2,1,0:T(8,128)(2,1)S(1)} all-to-all(bf16[32,128,128]{2,1,0:T(8,128)(2,1)S(1)} %main_attention.1), channel_id=1, replica_groups=mesh['grp'=4,'seq'=32] {'seq'}, dimensions={0} | all-to-all | bytes 2097152 | tf_op jit(solution)/shard_map/all_to_all | solution.py:265
  135.9 1.2 unpack.1
Async XLA Ops:
  0.0 11.1 %copy-start.4 = (f32[4096]{0:T(1024)S(1)}, f32[4096]{0:T(1024)}, u32[]{:S(2)}) copy-start(f32[4096]{0:T(1024)} %param.18) | copy-start | bytes 49156
  0.0 11.1 %copy-start.3 = (f32[4096]{0:T(1024)S(1)}, f32[4096]{0:T(1024)}, u32[]{:S(2)}) copy-start(f32[4096]{0:T(1024)} %param.17) | copy-start | bytes 49156
  0.0 11.1 %copy-start.2 = (bf16[1,128,4096]{2,1,0:T(8,128)(2,1)S(1)}, bf16[1,128,4096]{2,1,0:T(8,128)(2,1)}, u32[]{:S(2)}) copy-start(bf16[1,128,4096]{2,1,0:T(8,128)(2,1)} %param.16) | copy-start | bytes 3145732
  0.0 11.1 %copy-start.1 = (bf16[1,128,4096]{2,1,0:T(8,128)(2,1)S(1)}, bf16[1,128,4096]{2,1,0:T(8,128)(2,1)}, u32[]{:S(2)}) copy-start(bf16[1,128,4096]{2,1,0:T(8,128)(2,1)} %param.15) | copy-start | bytes 3145732
  0.0 11.1 %copy-start = (bf16[1,128,4096]{2,1,0:T(8,128)(2,1)S(1)}, bf16[1,128,4096]{2,1,0:T(8,128)(2,1)}, u32[]{:S(2)}) copy-start(bf16[1,128,4096]{2,1,0:T(8,128)(2,1)} %param.14) | copy-start | bytes 3145732
  2.6 23.9 %all-to-all-start = ((bf16[32,112,128]{2,1,0:T(8,128)(2,1)}), bf16[32,112,128]{2,1,0:T(8,128)(2,1)}, u32[]{:S(2)}, u32[]{:S(2)}) async-start(bf16[32,112,128]{2,1,0:T(8,128)(2,1)} %pack_ctrl.1), calls=%async_computation | async-start | bytes 1835008 | tf_op jit(solution)/shard_map/all_to_all | solution.py:265
  14.4 16.5 %copy-start.6 = (s32[1,8]{1,0:T(1,128)S(1)}, s32[1,8]{1,0:T(1,128)}, u32[]{:S(2)}) copy-start(s32[1,8]{1,0:T(1,128)} %param.25) | copy-start | bytes 100
  14.4 16.6 %copy-start.5 = (f32[16,4096]{1,0:T(8,128)S(1)}, f32[16,4096]{1,0:T(8,128)}, u32[]{:S(2)}) copy-start(f32[16,4096]{1,0:T(8,128)} %table.1) | copy-start | bytes 786436
  26.5 42.7 %all-to-all-start.1 = ((bf16[32,384,128]{2,1,0:T(8,128)(2,1)}), bf16[32,384,128]{2,1,0:T(8,128)(2,1)S(1)}, u32[]{:S(2)}, u32[]{:S(2)}) async-start(bf16[32,384,128]{2,1,0:T(8,128)(2,1)} %pack_main.1), calls=%async_computation.1 | async-start | bytes 6291456 | tf_op jit(solution)/shard_map/all_to_all | solution.py:265
  36.0 31.3 %collective-permute-start = (bf16[128,1024]{1,0:T(8,128)(2,1)S(1)}, bf16[128,1024]{1,0:T(8,128)(2,1)S(1)}, u32[]{:S(2)}, u32[]{:S(2)}) collective-permute-start(bf16[128,1024]{1,0:T(8,128)(2,1)S(1)} %get-tuple-element.9), channel_id=1, source_target_pairs={{96,0},{0,32},{32,64},{64,96},{97,1},{1,33},{33,65},{65,97},{98,2}... | collective-permute-start | bytes 786440 | tf_op jit(solution)/shard_map/ppermute | solution.py:332

commit v5 on v4

--- a/solution.py
+++ b/solution.py
@@ -25,7 +25,6 @@
 QB = 512
 KB = 1024
 PART = 256
-WIDE = 8
 VR = HEAD_DIM + 16
 SAFE = 2.0**100
 MIB = 1024 * 1024
@@ -104,7 +103,7 @@
 
 
 def main_kernel(
-    ends_ref, second, hint, notes_hbm, out, notes, match, gates, v_t, acc, sums, top_ref, sem
+    ends_ref, second, hint, notes_hbm, out, notes, match, gates, v_t, k_mark, acc, sums, top_ref, sem
 ):
     copy = pltpu.make_async_copy(notes_hbm, notes, sem)
     copy.start()
@@ -118,6 +117,15 @@
 
     for block in range(HEADS):
         v_t[:HEAD_DIM, block * 128 : block * 128 + 128] = second[block, 2 * TOK_DEV :, :]
+    lane = lax.broadcasted_iota(jnp.int32, (1, 128), 1)
+    marks = jnp.full((1, 128), SEQ, jnp.int32)
+    for f in range(FRAMES):
+        marks = jnp.where(lane == f, ends[f], marks)
+    for block in range(HEADS):
+        rows = slice(block * TOK_DEV, (block + 1) * TOK_DEV)
+        k_mark[rows, :HEAD_DIM] = second[block, TOK_DEV : 2 * TOK_DEV, :]
+        token = lax.broadcasted_iota(jnp.int32, (TOK_DEV, 128), 0) + block * TOK_DEV
+        k_mark[rows, HEAD_DIM:] = jnp.where(token >= marks, 1.0, 0.0).astype(BF16)
     v_t[HEAD_DIM:, :] = jnp.ones((VR - HEAD_DIM, SEQ), BF16)
     copy.wait()
     for g in range(8):
@@ -166,27 +174,23 @@
 
     def quick_block(i, carry):
         base = i * QB
-        limit = limit_of(base)
         q_t = queries_of(i)
+        column = lax.broadcasted_iota(jnp.int32, (16, QB), 1) + base
+        frame = jnp.zeros((16, QB), jnp.int32)
+        for f in range(FRAMES - 1):
+            frame = jnp.where(column >= ends[f], f + 1, frame)
+        hide = jnp.where(lax.broadcasted_iota(jnp.int32, (16, QB), 0) == frame, -1e30, 0.0)
+        q_mark = jnp.concatenate(
+            [q_t, hide.astype(BF16), jnp.zeros((HEAD_DIM - 16, QB), BF16)], axis=0
+        )
 
         def run(count):
             finish(jnp.maximum(i - 1, 0), acc)
-            total = None
-            edge = max(0, count - 3 * QB // PART)
-            cuts = sorted({0, edge}) + [count]
-            for c, d in zip(cuts[:-1], cuts[1:]):
-                per = PART // TOK_DEV
-                keys = second[c * per : d * per, TOK_DEV : 2 * TOK_DEV, :]
-                keys = keys.reshape((d - c) * PART, HEAD_DIM)
-                expo = jnp.exp2(jnp.dot(keys, q_t, preferred_element_type=F32) * SCALE2)
-                if c >= edge:
-                    row = lax.broadcasted_iota(jnp.int32, expo.shape, 0)
-                    expo = jnp.where(row < limit - c * PART, expo, 0.0)
-                part = jnp.dot(
-                    v_t[:, c * PART : d * PART], expo.astype(BF16), preferred_element_type=F32
-                )
-                total = part if total is None else total + part
-            acc[...] = total
+            keys = k_mark[: count * PART, :]
+            expo = jnp.exp2(jnp.dot(keys, q_mark, preferred_element_type=F32) * SCALE2)
+            acc[...] = jnp.dot(
+                v_t[:, : count * PART], expo.astype(BF16), preferred_element_type=F32
+            )
 
         parts = (end_of(base + QB - 1) + PART - 1) // PART
         for count in range(1, SEQ // PART + 1):
@@ -250,6 +254,7 @@
             pltpu.VMEM((CTRL, 128), F32),
             pltpu.VMEM((FRAMES, HEAD_DIM, 128), F32),
             pltpu.VMEM((VR, SEQ), BF16),
+            pltpu.VMEM((SEQ, 2 * HEAD_DIM), BF16),
             pltpu.VMEM((VR, QB), F32),
             pltpu.VMEM((SEQ // QB, QB), F32),
             pltpu.VMEM((8, QB), F32),

time: 137 us -> 136 us (level); the launches traced: 137 us -> 133 us
  blocking collectives: 49.2 us -> 20.1 us
  Pallas kernels: 29.5 us -> 54.7 us
    all_to_all x1, blocking collectives: 49.2 us -> 20.1 us  [exchange(): return lax.all_to_all(block, 'seq', split_axis=0, concat_axis=0, tiled=True)]
    pallas_call x1, Pallas kernels: 17.5 us -> 42.7 us  [run_main(): pl.pallas_call(main_kernel, out_shape=shape(HEADS, TOK_DEV, HEAD_DIM), in...]
where the time goes in v5:
time: 136 us; the launch traced here: 133 us
  Pallas kernels  54.7 us (40%)
  waiting for transfers between devices  45.3 us (33%)
  blocking collectives  20.1 us (15%)
  starting transfers between devices  12.9 us (9%)
    pallas_call x1, Pallas kernels, run_main(): pl.pallas_call(main_kernel, out_shape=shape(HEADS, TOK_DEV, HEAD_DIM), in...  42.7 us
    ppermute x1, waiting for transfers between devices, body(): lax.ppermute(hint, 'grp', [((i - 1) % groups, i) for i in range(groups)])  31.3 us
    all_to_all x1, blocking collectives, exchange(): return lax.all_to_all(block, 'seq', split_axis=0, concat_axis=0, tiled=True)  20.1 us
    all_to_all x2, waiting for transfers between devices, exchange(): return lax.all_to_all(block, 'seq', split_axis=0, concat_axis=0, tiled=True)  14 us
    all_to_all x2, starting transfers between devices, exchange(): return lax.all_to_all(block, 'seq', split_axis=0, concat_axis=0, tiled=True)  12.8 us
    pallas_call x1, Pallas kernels, body(): pl.pallas_call(ctrl_kernel, grid_spec=pltpu.PrefetchScalarGridSpec(num_sc...  4.97 us
    pallas_call x1, Pallas kernels, body(): pl.pallas_call(pack_main_kernel, out_shape=shape(HEADS, ROWS, HEAD_DIM),...  3.26 us
  transfers between devices with their start and end apart: 3, of which 3 were waited for; matrix products, arithmetic and copies ran while one was open for 0% of the time, Pallas kernels for 6%

profile of v5, /device:TPU:64, one launch (start us, length us, event | category | flops | bytes accessed | tf_op | source)
XLA Modules:
  0.0 133.2 jit_solution(3039272019173902552)
XLA Ops:
  0.0 0.0 copy-start.4
  0.0 0.0 copy-start.3
  0.0 0.0 copy-start.2
  0.0 0.0 copy-start.1
  0.0 0.0 copy-start
  0.0 2.5 %pack_ctrl.1 = bf16[32,112,128]{2,1,0:T(8,128)(2,1)} custom-call(bf16[32,4096]{1,0:T(8,128)(2,1)} %bitcast.18, bf16[32,4096]{1,0:T(8,128)(2,1)} %bitcast.19, bf16[32,4096]{1,0:T(8,128)(2,1)} %bitcast.20, f32[1,4096]{1,0:T(1,128)} %bitcast.21, f32[1,4096]{1,0:T(1,128)} %bitcast.22, s32[1,128]{1,0:T(1,128)} %frames.1, s32[1,32]{1,0:T(1,128)} %match.1), custom_call_target="tpu_custom_call" | custom-call | flops 2000000 | bytes 2000000 | tf_op jit(solution)/shard_map/pack_ctrl/pallas_call | solution.py:289
  2.6 8.5 %all-to-all-start = ((bf16[32,112,128]{2,1,0:T(8,128)(2,1)}), bf16[32,112,128]{2,1,0:T(8,128)(2,1)}, u32[]{:S(2)}, u32[]{:S(2)}) async-start(bf16[32,112,128]{2,1,0:T(8,128)(2,1)} %pack_ctrl.1), calls=%async_computation | async-start | bytes 1835008 | tf_op jit(solution)/shard_map/all_to_all | solution.py:270
  11.1 0.0 copy-done.4
  11.1 0.0 copy-done.3
  11.1 0.0 copy-done.2
  11.1 0.0 copy-done.1
  11.1 0.0 copy-done
  11.1 3.3 %pack_main.1 = bf16[32,384,128]{2,1,0:T(8,128)(2,1)} custom-call(bf16[128,4096]{1,0:T(8,128)(2,1)S(1)} %bitcast.13, bf16[128,4096]{1,0:T(8,128)(2,1)S(1)} %bitcast.14, bf16[128,4096]{1,0:T(8,128)(2,1)S(1)} %bitcast.15, f32[1,4096]{1,0:T(1,128)S(1)} %bitcast.16, f32[1,4096]{1,0:T(1,128)S(1)} %bitcast.17), custom_call_target="tpu_custom_call" | custom-call | flops 8000000 | bytes 6000000 | tf_op jit(solution)/shard_map/pack_main/pallas_call | solution.py:307
  14.4 0.0 copy-start.6
  14.4 0.0 copy-start.5
  14.4 12.1 %all-to-all-done.first = bf16[32,112,128]{2,1,0:T(8,128)(2,1)} async-done(((bf16[32,112,128]{2,1,0:T(8,128)(2,1)}), bf16[32,112,128]{2,1,0:T(8,128)(2,1)}, u32[]{:S(2)}, u32[]{:S(2)}) %all-to-all-start) | async-done | bytes 917536 | tf_op jit(solution)/shard_map/all_to_all | solution.py:270
  26.5 4.3 %all-to-all-start.1 = ((bf16[32,384,128]{2,1,0:T(8,128)(2,1)}), bf16[32,384,128]{2,1,0:T(8,128)(2,1)S(1)}, u32[]{:S(2)}, u32[]{:S(2)}) async-start(bf16[32,384,128]{2,1,0:T(8,128)(2,1)} %pack_main.1), calls=%async_computation.1 | async-start | bytes 6291456 | tf_op jit(solution)/shard_map/all_to_all | solution.py:270
  30.9 0.0 copy-done.6
  30.9 0.1 pad_add_fusion.places
  31.0 0.0 copy-done.5
  31.0 5.0 %ctrl_attention.1 = (bf16[128,1024]{1,0:T(8,128)(2,1)S(1)}, s32[8]{0:T(128)S(1)}, f32[16,128]{1,0:T(8,128)S(1)}) custom-call(s32[9]{0:T(128)S(1)} %pad_add_fusion.places, f32[16,4096]{1,0:T(8,128)S(1)} %copy-done.5, bf16[32,112,128]{2,1,0:T(8,128)(2,1)} %all-to-all-done.first), custom_call_target="tpu_custom_call" | custom-call | flops 536870912 | bytes 1000000 | tf_op jit(solution)/shard_map/ctrl_attention/pallas_call | solution.py:319
  36.0 0.1 collective-permute-start
  36.0 31.3 %collective-permute-done.hint = bf16[128,1024]{1,0:T(8,128)(2,1)S(1)} collective-permute-done((bf16[128,1024]{1,0:T(8,128)(2,1)S(1)}, bf16[128,1024]{1,0:T(8,128)(2,1)S(1)}, u32[]{:S(2)}, u32[]{:S(2)}) %collective-permute-start) | collective-permute-done | bytes 262176 | tf_op jit(solution)/shard_map/ppermute | solution.py:337
  67.3 1.9 %all-to-all-done.1.second = bf16[32,384,128]{2,1,0:T(8,128)(2,1)S(1)} async-done(((bf16[32,384,128]{2,1,0:T(8,128)(2,1)}), bf16[32,384,128]{2,1,0:T(8,128)(2,1)S(1)}, u32[]{:S(2)}, u32[]{:S(2)}) %all-to-all-start.1) | async-done | bytes 3145760 | tf_op jit(solution)/shard_map/all_to_all | solution.py:270
  69.2 42.7 %main_attention.1 = bf16[32,128,128]{2,1,0:T(8,128)(2,1)S(1)} custom-call(s32[8]{0:T(128)S(1)} %get-tuple-element.8.ends_ref, bf16[32,384,128]{2,1,0:T(8,128)(2,1)S(1)} %all-to-all-done.1.second, bf16[128,1024]{1,0:T(8,128)(2,1)S(1)} %collective-permute-done.hint, f32[16,128]{1,0:T(8,128)S(1)} %get-tuple-element.10.notes_hbm), custom_call_target="tpu_custom_call" | custom-call | flops 8589934592 | bytes 5000000 | tf_op jit(solution)/shard_map/main_attention/pallas_call | solution.py:247
  111.9 20.1 %all_to_all.15.rows = bf16[32,128,128]{2,1,0:T(8,128)(2,1)S(1)} all-to-all(bf16[32,128,128]{2,1,0:T(8,128)(2,1)S(1)} %main_attention.1), channel_id=1, replica_groups=mesh['grp'=4,'seq'=32] {'seq'}, dimensions={0} | all-to-all | bytes 2097152 | tf_op jit(solution)/shard_map/all_to_all | solution.py:270
  132.0 1.2 unpack.1
Async XLA Ops:
  0.0 11.1 %copy-start.4 = (f32[4096]{0:T(1024)S(1)}, f32[4096]{0:T(1024)}, u32[]{:S(2)}) copy-start(f32[4096]{0:T(1024)} %param.18) | copy-start | bytes 49156
  0.0 11.1 %copy-start.3 = (f32[4096]{0:T(1024)S(1)}, f32[4096]{0:T(1024)}, u32[]{:S(2)}) copy-start(f32[4096]{0:T(1024)} %param.17) | copy-start | bytes 49156
  0.0 11.1 %copy-start.2 = (bf16[1,128,4096]{2,1,0:T(8,128)(2,1)S(1)}, bf16[1,128,4096]{2,1,0:T(8,128)(2,1)}, u32[]{:S(2)}) copy-start(bf16[1,128,4096]{2,1,0:T(8,128)(2,1)} %param.16) | copy-start | bytes 3145732
  0.0 11.1 %copy-start.1 = (bf16[1,128,4096]{2,1,0:T(8,128)(2,1)S(1)}, bf16[1,128,4096]{2,1,0:T(8,128)(2,1)}, u32[]{:S(2)}) copy-start(bf16[1,128,4096]{2,1,0:T(8,128)(2,1)} %param.15) | copy-start | bytes 3145732
  0.0 11.1 %copy-start = (bf16[1,128,4096]{2,1,0:T(8,128)(2,1)S(1)}, bf16[1,128,4096]{2,1,0:T(8,128)(2,1)}, u32[]{:S(2)}) copy-start(bf16[1,128,4096]{2,1,0:T(8,128)(2,1)} %param.14) | copy-start | bytes 3145732
  2.6 23.9 %all-to-all-start = ((bf16[32,112,128]{2,1,0:T(8,128)(2,1)}), bf16[32,112,128]{2,1,0:T(8,128)(2,1)}, u32[]{:S(2)}, u32[]{:S(2)}) async-start(bf16[32,112,128]{2,1,0:T(8,128)(2,1)} %pack_ctrl.1), calls=%async_computation | async-start | bytes 1835008 | tf_op jit(solution)/shard_map/all_to_all | solution.py:270
  14.4 16.5 %copy-start.6 = (s32[1,8]{1,0:T(1,128)S(1)}, s32[1,8]{1,0:T(1,128)}, u32[]{:S(2)}) copy-start(s32[1,8]{1,0:T(1,128)} %param.25) | copy-start | bytes 100
  14.4 16.6 %copy-start.5 = (f32[16,4096]{1,0:T(8,128)S(1)}, f32[16,4096]{1,0:T(8,128)}, u32[]{:S(2)}) copy-start(f32[16,4096]{1,0:T(8,128)} %table.1) | copy-start | bytes 786436
  26.5 42.7 %all-to-all-start.1 = ((bf16[32,384,128]{2,1,0:T(8,128)(2,1)}), bf16[32,384,128]{2,1,0:T(8,128)(2,1)S(1)}, u32[]{:S(2)}, u32[]{:S(2)}) async-start(bf16[32,384,128]{2,1,0:T(8,128)(2,1)} %pack_main.1), calls=%async_computation.1 | async-start | bytes 6291456 | tf_op jit(solution)/shard_map/all_to_all | solution.py:270
  36.0 31.3 %collective-permute-start = (bf16[128,1024]{1,0:T(8,128)(2,1)S(1)}, bf16[128,1024]{1,0:T(8,128)(2,1)S(1)}, u32[]{:S(2)}, u32[]{:S(2)}) collective-permute-start(bf16[128,1024]{1,0:T(8,128)(2,1)S(1)} %get-tuple-element.9), channel_id=1, source_target_pairs={{96,0},{0,32},{32,64},{64,96},{97,1},{1,33},{33,65},{65,97},{98,2}... | collective-permute-start | bytes 786440 | tf_op jit(solution)/shard_map/ppermute | solution.py:337

commit v6 on v5

--- a/solution.py
+++ b/solution.py
@@ -1,4 +1,3 @@
-import functools
 import math
 
 import jax
@@ -193,8 +192,16 @@
             )
 
         parts = (end_of(base + QB - 1) + PART - 1) // PART
-        for count in range(1, SEQ // PART + 1):
-            pl.when(parts == count)(functools.partial(run, count))
+        def choose(low, high):
+            if low == high:
+                run(low)
+                return
+            middle = (low + high) // 2
+            lax.cond(
+                parts <= middle, lambda: choose(low, middle), lambda: choose(middle + 1, high)
+            )
+
+        choose(1, SEQ // PART)
 
         sums[pl.ds(i, 1), :] = acc[HEAD_DIM : HEAD_DIM + 1, :]
         return carry

time: 136 us -> 135 us (level)
  blocking collectives: 20.1 us -> 48.8 us
  Pallas kernels: 54.7 us -> 26.1 us
    all_to_all x1, blocking collectives: 20.1 us -> 48.8 us  [exchange(): return lax.all_to_all(block, 'seq', split_axis=0, concat_axis=0, tiled=True)]
    pallas_call x1, Pallas kernels: 42.7 us -> 14.1 us  [run_main(): pl.pallas_call(main_kernel, out_shape=shape(HEADS, TOK_DEV, HEAD_DIM), in...]
where the time goes in v6:
time: 135 us; the launch traced here: 133 us
  blocking collectives  48.8 us (36%)
  waiting for transfers between devices  45.3 us (34%)
  Pallas kernels  26.1 us (19%)
  starting transfers between devices  12.9 us (10%)
    all_to_all x1, blocking collectives, exchange(): return lax.all_to_all(block, 'seq', split_axis=0, concat_axis=0, tiled=True)  48.8 us
    ppermute x1, waiting for transfers between devices, body(): lax.ppermute(hint, 'grp', [((i - 1) % groups, i) for i in range(groups)])  31.3 us
    pallas_call x1, Pallas kernels, run_main(): pl.pallas_call(main_kernel, out_shape=shape(HEADS, TOK_DEV, HEAD_DIM), in...  14.1 us
    all_to_all x2, waiting for transfers between devices, exchange(): return lax.all_to_all(block, 'seq', split_axis=0, concat_axis=0, tiled=True)  14 us
    all_to_all x2, starting transfers between devices, exchange(): return lax.all_to_all(block, 'seq', split_axis=0, concat_axis=0, tiled=True)  12.8 us
    pallas_call x1, Pallas kernels, body(): pl.pallas_call(ctrl_kernel, grid_spec=pltpu.PrefetchScalarGridSpec(num_sc...  4.97 us
    pallas_call x1, Pallas kernels, body(): pl.pallas_call(pack_main_kernel, out_shape=shape(HEADS, ROWS, HEAD_DIM),...  3.26 us
  transfers between devices with their start and end apart: 3, of which 3 were waited for; matrix products, arithmetic and copies ran while one was open for 0% of the time, Pallas kernels for 6%

profile of v6, /device:TPU:64, one launch (start us, length us, event | category | flops | bytes accessed | tf_op | source)
XLA Modules:
  0.0 133.3 jit_solution(17273453936910730406)
XLA Ops:
  0.0 0.0 copy-start.4
  0.0 0.0 copy-start.3
  0.0 0.0 copy-start.2
  0.0 0.0 copy-start.1
  0.0 0.0 copy-start
  0.0 2.5 %pack_ctrl.1 = bf16[32,112,128]{2,1,0:T(8,128)(2,1)} custom-call(bf16[32,4096]{1,0:T(8,128)(2,1)} %bitcast.18, bf16[32,4096]{1,0:T(8,128)(2,1)} %bitcast.19, bf16[32,4096]{1,0:T(8,128)(2,1)} %bitcast.20, f32[1,4096]{1,0:T(1,128)} %bitcast.21, f32[1,4096]{1,0:T(1,128)} %bitcast.22, s32[1,128]{1,0:T(1,128)} %frames.1, s32[1,32]{1,0:T(1,128)} %match.1), custom_call_target="tpu_custom_call" | custom-call | flops 2000000 | bytes 2000000 | tf_op jit(solution)/shard_map/pack_ctrl/pallas_call | solution.py:296
  2.6 8.5 %all-to-all-start = ((bf16[32,112,128]{2,1,0:T(8,128)(2,1)}), bf16[32,112,128]{2,1,0:T(8,128)(2,1)}, u32[]{:S(2)}, u32[]{:S(2)}) async-start(bf16[32,112,128]{2,1,0:T(8,128)(2,1)} %pack_ctrl.1), calls=%async_computation | async-start | bytes 1835008 | tf_op jit(solution)/shard_map/all_to_all | solution.py:277
  11.1 0.0 copy-done.4
  11.1 0.0 copy-done.3
  11.1 0.0 copy-done.2
  11.1 0.0 copy-done.1
  11.1 0.0 copy-done
  11.1 3.3 %pack_main.1 = bf16[32,384,128]{2,1,0:T(8,128)(2,1)} custom-call(bf16[128,4096]{1,0:T(8,128)(2,1)S(1)} %bitcast.13, bf16[128,4096]{1,0:T(8,128)(2,1)S(1)} %bitcast.14, bf16[128,4096]{1,0:T(8,128)(2,1)S(1)} %bitcast.15, f32[1,4096]{1,0:T(1,128)S(1)} %bitcast.16, f32[1,4096]{1,0:T(1,128)S(1)} %bitcast.17), custom_call_target="tpu_custom_call" | custom-call | flops 8000000 | bytes 6000000 | tf_op jit(solution)/shard_map/pack_main/pallas_call | solution.py:314
  14.4 0.0 copy-start.6
  14.4 0.0 copy-start.5
  14.4 12.1 %all-to-all-done.first = bf16[32,112,128]{2,1,0:T(8,128)(2,1)} async-done(((bf16[32,112,128]{2,1,0:T(8,128)(2,1)}), bf16[32,112,128]{2,1,0:T(8,128)(2,1)}, u32[]{:S(2)}, u32[]{:S(2)}) %all-to-all-start) | async-done | bytes 917536 | tf_op jit(solution)/shard_map/all_to_all | solution.py:277
  26.5 4.3 %all-to-all-start.1 = ((bf16[32,384,128]{2,1,0:T(8,128)(2,1)}), bf16[32,384,128]{2,1,0:T(8,128)(2,1)S(1)}, u32[]{:S(2)}, u32[]{:S(2)}) async-start(bf16[32,384,128]{2,1,0:T(8,128)(2,1)} %pack_main.1), calls=%async_computation.1 | async-start | bytes 6291456 | tf_op jit(solution)/shard_map/all_to_all | solution.py:277
  30.9 0.0 copy-done.6
  30.9 0.1 pad_add_fusion.places
  31.0 0.0 copy-done.5
  31.0 5.0 %ctrl_attention.1 = (bf16[128,1024]{1,0:T(8,128)(2,1)S(1)}, s32[8]{0:T(128)S(1)}, f32[16,128]{1,0:T(8,128)S(1)}) custom-call(s32[9]{0:T(128)S(1)} %pad_add_fusion.places, f32[16,4096]{1,0:T(8,128)S(1)} %copy-done.5, bf16[32,112,128]{2,1,0:T(8,128)(2,1)} %all-to-all-done.first), custom_call_target="tpu_custom_call" | custom-call | flops 536870912 | bytes 1000000 | tf_op jit(solution)/shard_map/ctrl_attention/pallas_call | solution.py:326
  36.0 0.1 collective-permute-start
  36.0 31.3 %collective-permute-done.hint = bf16[128,1024]{1,0:T(8,128)(2,1)S(1)} collective-permute-done((bf16[128,1024]{1,0:T(8,128)(2,1)S(1)}, bf16[128,1024]{1,0:T(8,128)(2,1)S(1)}, u32[]{:S(2)}, u32[]{:S(2)}) %collective-permute-start) | collective-permute-done | bytes 262176 | tf_op jit(solution)/shard_map/ppermute | solution.py:344
  67.3 1.9 %all-to-all-done.1.second = bf16[32,384,128]{2,1,0:T(8,128)(2,1)S(1)} async-done(((bf16[32,384,128]{2,1,0:T(8,128)(2,1)}), bf16[32,384,128]{2,1,0:T(8,128)(2,1)S(1)}, u32[]{:S(2)}, u32[]{:S(2)}) %all-to-all-start.1) | async-done | bytes 3145760 | tf_op jit(solution)/shard_map/all_to_all | solution.py:277
  69.2 14.1 %main_attention.1 = bf16[32,128,128]{2,1,0:T(8,128)(2,1)S(1)} custom-call(s32[8]{0:T(128)S(1)} %get-tuple-element.8.ends_ref, bf16[32,384,128]{2,1,0:T(8,128)(2,1)S(1)} %all-to-all-done.1.second, bf16[128,1024]{1,0:T(8,128)(2,1)S(1)} %collective-permute-done.hint, f32[16,128]{1,0:T(8,128)S(1)} %get-tuple-element.10.notes_hbm), custom_call_target="tpu_custom_call" | custom-call | flops 8589934592 | bytes 5000000 | tf_op jit(solution)/shard_map/main_attention/pallas_call | solution.py:254
  83.3 48.8 %all_to_all.15.rows = bf16[32,128,128]{2,1,0:T(8,128)(2,1)S(1)} all-to-all(bf16[32,128,128]{2,1,0:T(8,128)(2,1)S(1)} %main_attention.1), channel_id=1, replica_groups=mesh['grp'=4,'seq'=32] {'seq'}, dimensions={0} | all-to-all | bytes 2097152 | tf_op jit(solution)/shard_map/all_to_all | solution.py:277
  132.0 1.2 unpack.1
Async XLA Ops:
  0.0 11.1 %copy-start.4 = (f32[4096]{0:T(1024)S(1)}, f32[4096]{0:T(1024)}, u32[]{:S(2)}) copy-start(f32[4096]{0:T(1024)} %param.18) | copy-start | bytes 49156
  0.0 11.1 %copy-start.3 = (f32[4096]{0:T(1024)S(1)}, f32[4096]{0:T(1024)}, u32[]{:S(2)}) copy-start(f32[4096]{0:T(1024)} %param.17) | copy-start | bytes 49156
  0.0 11.1 %copy-start.2 = (bf16[1,128,4096]{2,1,0:T(8,128)(2,1)S(1)}, bf16[1,128,4096]{2,1,0:T(8,128)(2,1)}, u32[]{:S(2)}) copy-start(bf16[1,128,4096]{2,1,0:T(8,128)(2,1)} %param.16) | copy-start | bytes 3145732
  0.0 11.1 %copy-start.1 = (bf16[1,128,4096]{2,1,0:T(8,128)(2,1)S(1)}, bf16[1,128,4096]{2,1,0:T(8,128)(2,1)}, u32[]{:S(2)}) copy-start(bf16[1,128,4096]{2,1,0:T(8,128)(2,1)} %param.15) | copy-start | bytes 3145732
  0.0 11.1 %copy-start = (bf16[1,128,4096]{2,1,0:T(8,128)(2,1)S(1)}, bf16[1,128,4096]{2,1,0:T(8,128)(2,1)}, u32[]{:S(2)}) copy-start(bf16[1,128,4096]{2,1,0:T(8,128)(2,1)} %param.14) | copy-start | bytes 3145732
  2.6 23.9 %all-to-all-start = ((bf16[32,112,128]{2,1,0:T(8,128)(2,1)}), bf16[32,112,128]{2,1,0:T(8,128)(2,1)}, u32[]{:S(2)}, u32[]{:S(2)}) async-start(bf16[32,112,128]{2,1,0:T(8,128)(2,1)} %pack_ctrl.1), calls=%async_computation | async-start | bytes 1835008 | tf_op jit(solution)/shard_map/all_to_all | solution.py:277
  14.4 16.5 %copy-start.6 = (s32[1,8]{1,0:T(1,128)S(1)}, s32[1,8]{1,0:T(1,128)}, u32[]{:S(2)}) copy-start(s32[1,8]{1,0:T(1,128)} %param.25) | copy-start | bytes 100
  14.4 16.6 %copy-start.5 = (f32[16,4096]{1,0:T(8,128)S(1)}, f32[16,4096]{1,0:T(8,128)}, u32[]{:S(2)}) copy-start(f32[16,4096]{1,0:T(8,128)} %table.1) | copy-start | bytes 786436
  26.5 42.7 %all-to-all-start.1 = ((bf16[32,384,128]{2,1,0:T(8,128)(2,1)}), bf16[32,384,128]{2,1,0:T(8,128)(2,1)S(1)}, u32[]{:S(2)}, u32[]{:S(2)}) async-start(bf16[32,384,128]{2,1,0:T(8,128)(2,1)} %pack_main.1), calls=%async_computation.1 | async-start | bytes 6291456 | tf_op jit(solution)/shard_map/all_to_all | solution.py:277
  36.0 31.3 %collective-permute-start = (bf16[128,1024]{1,0:T(8,128)(2,1)S(1)}, bf16[128,1024]{1,0:T(8,128)(2,1)S(1)}, u32[]{:S(2)}, u32[]{:S(2)}) collective-permute-start(bf16[128,1024]{1,0:T(8,128)(2,1)S(1)} %get-tuple-element.9), channel_id=1, source_target_pairs={{96,0},{0,32},{32,64},{64,96},{97,1},{1,33},{33,65},{65,97},{98,2}... | collective-permute-start | bytes 786440 | tf_op jit(solution)/shard_map/ppermute | solution.py:344

commit v7 on v6

--- a/solution.py
+++ b/solution.py
@@ -122,9 +122,8 @@
         marks = jnp.where(lane == f, ends[f], marks)
     for block in range(HEADS):
         rows = slice(block * TOK_DEV, (block + 1) * TOK_DEV)
-        k_mark[rows, :HEAD_DIM] = second[block, TOK_DEV : 2 * TOK_DEV, :]
         token = lax.broadcasted_iota(jnp.int32, (TOK_DEV, 128), 0) + block * TOK_DEV
-        k_mark[rows, HEAD_DIM:] = jnp.where(token >= marks, 1.0, 0.0).astype(BF16)
+        k_mark[rows, :] = jnp.where(token >= marks, 1.0, 0.0).astype(BF16)
     v_t[HEAD_DIM:, :] = jnp.ones((VR - HEAD_DIM, SEQ), BF16)
     copy.wait()
     for g in range(8):
@@ -185,7 +184,10 @@
 
         def run(count):
             finish(jnp.maximum(i - 1, 0), acc)
-            keys = k_mark[: count * PART, :]
+            held = second[: count * PART // TOK_DEV, TOK_DEV : 2 * TOK_DEV, :]
+            keys = jnp.concatenate(
+                [held.reshape(count * PART, HEAD_DIM), k_mark[: count * PART, :]], axis=1
+            )
             expo = jnp.exp2(jnp.dot(keys, q_mark, preferred_element_type=F32) * SCALE2)
             acc[...] = jnp.dot(
                 v_t[:, : count * PART], expo.astype(BF16), preferred_element_type=F32
@@ -261,7 +263,7 @@
             pltpu.VMEM((CTRL, 128), F32),
             pltpu.VMEM((FRAMES, HEAD_DIM, 128), F32),
             pltpu.VMEM((VR, SEQ), BF16),
-            pltpu.VMEM((SEQ, 2 * HEAD_DIM), BF16),
+            pltpu.VMEM((SEQ, HEAD_DIM), BF16),
             pltpu.VMEM((VR, QB), F32),
             pltpu.VMEM((SEQ // QB, QB), F32),
             pltpu.VMEM((8, QB), F32),

time: 135 us -> 135 us (level)
  blocking collectives: 48.8 us -> 47.3 us
    all_to_all x1, blocking collectives: 48.8 us -> 47.3 us  [exchange(): return lax.all_to_all(block, 'seq', split_axis=0, concat_axis=0, tiled=True)]
where the time goes in v7:
time: 135 us; the launch traced here: 132 us
  blocking collectives  47.3 us (35%)
  waiting for transfers between devices  45.3 us (34%)
  Pallas kernels  26.3 us (19%)
  starting transfers between devices  12.9 us (10%)
    all_to_all x1, blocking collectives, exchange(): return lax.all_to_all(block, 'seq', split_axis=0, concat_axis=0, tiled=True)  47.3 us
    ppermute x1, waiting for transfers between devices, body(): lax.ppermute(hint, 'grp', [((i - 1) % groups, i) for i in range(groups)])  31.3 us
    pallas_call x1, Pallas kernels, run_main(): pl.pallas_call(main_kernel, out_shape=shape(HEADS, TOK_DEV, HEAD_DIM), in...  14.2 us
    all_to_all x2, waiting for transfers between devices, exchange(): return lax.all_to_all(block, 'seq', split_axis=0, concat_axis=0, tiled=True)  14 us
    all_to_all x2, starting transfers between devices, exchange(): return lax.all_to_all(block, 'seq', split_axis=0, concat_axis=0, tiled=True)  12.8 us
    pallas_call x1, Pallas kernels, body(): pl.pallas_call(ctrl_kernel, grid_spec=pltpu.PrefetchScalarGridSpec(num_sc...  4.97 us
    pallas_call x1, Pallas kernels, body(): pl.pallas_call(pack_main_kernel, out_shape=shape(HEADS, ROWS, HEAD_DIM),...  3.26 us
  transfers between devices with their start and end apart: 3, of which 3 were waited for; matrix products, arithmetic and copies ran while one was open for 0% of the time, Pallas kernels for 6%

profile of v7, /device:TPU:64, one launch (start us, length us, event | category | flops | bytes accessed | tf_op | source)
XLA Modules:
  0.0 131.9 jit_solution(7244987908379832907)
XLA Ops:
  0.0 0.0 copy-start.4
  0.0 0.0 copy-start.3
  0.0 0.0 copy-start.2
  0.0 0.0 copy-start.1
  0.0 0.0 copy-start
  0.0 2.5 %pack_ctrl.1 = bf16[32,112,128]{2,1,0:T(8,128)(2,1)} custom-call(bf16[32,4096]{1,0:T(8,128)(2,1)} %bitcast.18, bf16[32,4096]{1,0:T(8,128)(2,1)} %bitcast.19, bf16[32,4096]{1,0:T(8,128)(2,1)} %bitcast.20, f32[1,4096]{1,0:T(1,128)} %bitcast.21, f32[1,4096]{1,0:T(1,128)} %bitcast.22, s32[1,128]{1,0:T(1,128)} %frames.1, s32[1,32]{1,0:T(1,128)} %match.1), custom_call_target="tpu_custom_call" | custom-call | flops 2000000 | bytes 2000000 | tf_op jit(solution)/shard_map/pack_ctrl/pallas_call | solution.py:298
  2.6 8.5 %all-to-all-start = ((bf16[32,112,128]{2,1,0:T(8,128)(2,1)}), bf16[32,112,128]{2,1,0:T(8,128)(2,1)}, u32[]{:S(2)}, u32[]{:S(2)}) async-start(bf16[32,112,128]{2,1,0:T(8,128)(2,1)} %pack_ctrl.1), calls=%async_computation | async-start | bytes 1835008 | tf_op jit(solution)/shard_map/all_to_all | solution.py:279
  11.1 0.0 copy-done.4
  11.1 0.0 copy-done.3
  11.1 0.0 copy-done.2
  11.1 0.0 copy-done.1
  11.1 0.0 copy-done
  11.1 3.3 %pack_main.1 = bf16[32,384,128]{2,1,0:T(8,128)(2,1)} custom-call(bf16[128,4096]{1,0:T(8,128)(2,1)S(1)} %bitcast.13, bf16[128,4096]{1,0:T(8,128)(2,1)S(1)} %bitcast.14, bf16[128,4096]{1,0:T(8,128)(2,1)S(1)} %bitcast.15, f32[1,4096]{1,0:T(1,128)S(1)} %bitcast.16, f32[1,4096]{1,0:T(1,128)S(1)} %bitcast.17), custom_call_target="tpu_custom_call" | custom-call | flops 8000000 | bytes 6000000 | tf_op jit(solution)/shard_map/pack_main/pallas_call | solution.py:316
  14.4 0.0 copy-start.6
  14.4 0.0 copy-start.5
  14.4 12.1 %all-to-all-done.first = bf16[32,112,128]{2,1,0:T(8,128)(2,1)} async-done(((bf16[32,112,128]{2,1,0:T(8,128)(2,1)}), bf16[32,112,128]{2,1,0:T(8,128)(2,1)}, u32[]{:S(2)}, u32[]{:S(2)}) %all-to-all-start) | async-done | bytes 917536 | tf_op jit(solution)/shard_map/all_to_all | solution.py:279
  26.5 4.3 %all-to-all-start.1 = ((bf16[32,384,128]{2,1,0:T(8,128)(2,1)}), bf16[32,384,128]{2,1,0:T(8,128)(2,1)S(1)}, u32[]{:S(2)}, u32[]{:S(2)}) async-start(bf16[32,384,128]{2,1,0:T(8,128)(2,1)} %pack_main.1), calls=%async_computation.1 | async-start | bytes 6291456 | tf_op jit(solution)/shard_map/all_to_all | solution.py:279
  30.9 0.0 copy-done.6
  30.9 0.1 pad_add_fusion.places
  31.0 0.0 copy-done.5
  31.0 5.0 %ctrl_attention.1 = (bf16[128,1024]{1,0:T(8,128)(2,1)S(1)}, s32[8]{0:T(128)S(1)}, f32[16,128]{1,0:T(8,128)S(1)}) custom-call(s32[9]{0:T(128)S(1)} %pad_add_fusion.places, f32[16,4096]{1,0:T(8,128)S(1)} %copy-done.5, bf16[32,112,128]{2,1,0:T(8,128)(2,1)} %all-to-all-done.first), custom_call_target="tpu_custom_call" | custom-call | flops 536870912 | bytes 1000000 | tf_op jit(solution)/shard_map/ctrl_attention/pallas_call | solution.py:328
  36.0 0.1 collective-permute-start
  36.0 31.3 %collective-permute-done.hint = bf16[128,1024]{1,0:T(8,128)(2,1)S(1)} collective-permute-done((bf16[128,1024]{1,0:T(8,128)(2,1)S(1)}, bf16[128,1024]{1,0:T(8,128)(2,1)S(1)}, u32[]{:S(2)}, u32[]{:S(2)}) %collective-permute-start) | collective-permute-done | bytes 262176 | tf_op jit(solution)/shard_map/ppermute | solution.py:346
  67.3 1.9 %all-to-all-done.1.second = bf16[32,384,128]{2,1,0:T(8,128)(2,1)S(1)} async-done(((bf16[32,384,128]{2,1,0:T(8,128)(2,1)}), bf16[32,384,128]{2,1,0:T(8,128)(2,1)S(1)}, u32[]{:S(2)}, u32[]{:S(2)}) %all-to-all-start.1) | async-done | bytes 3145760 | tf_op jit(solution)/shard_map/all_to_all | solution.py:279
  69.2 14.2 %main_attention.1 = bf16[32,128,128]{2,1,0:T(8,128)(2,1)S(1)} custom-call(s32[8]{0:T(128)S(1)} %get-tuple-element.8.ends_ref, bf16[32,384,128]{2,1,0:T(8,128)(2,1)S(1)} %all-to-all-done.1.second, bf16[128,1024]{1,0:T(8,128)(2,1)S(1)} %collective-permute-done.hint, f32[16,128]{1,0:T(8,128)S(1)} %get-tuple-element.10.notes_hbm), custom_call_target="tpu_custom_call" | custom-call | flops 8589934592 | bytes 5000000 | tf_op jit(solution)/shard_map/main_attention/pallas_call | solution.py:256
  83.4 47.3 %all_to_all.15.rows = bf16[32,128,128]{2,1,0:T(8,128)(2,1)S(1)} all-to-all(bf16[32,128,128]{2,1,0:T(8,128)(2,1)S(1)} %main_attention.1), channel_id=1, replica_groups=mesh['grp'=4,'seq'=32] {'seq'}, dimensions={0} | all-to-all | bytes 2097152 | tf_op jit(solution)/shard_map/all_to_all | solution.py:279
  130.7 1.2 unpack.1
Async XLA Ops:
  0.0 11.1 %copy-start.4 = (f32[4096]{0:T(1024)S(1)}, f32[4096]{0:T(1024)}, u32[]{:S(2)}) copy-start(f32[4096]{0:T(1024)} %param.18) | copy-start | bytes 49156
  0.0 11.1 %copy-start.3 = (f32[4096]{0:T(1024)S(1)}, f32[4096]{0:T(1024)}, u32[]{:S(2)}) copy-start(f32[4096]{0:T(1024)} %param.17) | copy-start | bytes 49156
  0.0 11.1 %copy-start.2 = (bf16[1,128,4096]{2,1,0:T(8,128)(2,1)S(1)}, bf16[1,128,4096]{2,1,0:T(8,128)(2,1)}, u32[]{:S(2)}) copy-start(bf16[1,128,4096]{2,1,0:T(8,128)(2,1)} %param.16) | copy-start | bytes 3145732
  0.0 11.1 %copy-start.1 = (bf16[1,128,4096]{2,1,0:T(8,128)(2,1)S(1)}, bf16[1,128,4096]{2,1,0:T(8,128)(2,1)}, u32[]{:S(2)}) copy-start(bf16[1,128,4096]{2,1,0:T(8,128)(2,1)} %param.15) | copy-start | bytes 3145732
  0.0 11.1 %copy-start = (bf16[1,128,4096]{2,1,0:T(8,128)(2,1)S(1)}, bf16[1,128,4096]{2,1,0:T(8,128)(2,1)}, u32[]{:S(2)}) copy-start(bf16[1,128,4096]{2,1,0:T(8,128)(2,1)} %param.14) | copy-start | bytes 3145732
  2.6 23.9 %all-to-all-start = ((bf16[32,112,128]{2,1,0:T(8,128)(2,1)}), bf16[32,112,128]{2,1,0:T(8,128)(2,1)}, u32[]{:S(2)}, u32[]{:S(2)}) async-start(bf16[32,112,128]{2,1,0:T(8,128)(2,1)} %pack_ctrl.1), calls=%async_computation | async-start | bytes 1835008 | tf_op jit(solution)/shard_map/all_to_all | solution.py:279
  14.4 16.5 %copy-start.6 = (s32[1,8]{1,0:T(1,128)S(1)}, s32[1,8]{1,0:T(1,128)}, u32[]{:S(2)}) copy-start(s32[1,8]{1,0:T(1,128)} %param.25) | copy-start | bytes 100
  14.4 16.6 %copy-start.5 = (f32[16,4096]{1,0:T(8,128)S(1)}, f32[16,4096]{1,0:T(8,128)}, u32[]{:S(2)}) copy-start(f32[16,4096]{1,0:T(8,128)} %table.1) | copy-start | bytes 786436
  26.5 42.7 %all-to-all-start.1 = ((bf16[32,384,128]{2,1,0:T(8,128)(2,1)}), bf16[32,384,128]{2,1,0:T(8,128)(2,1)S(1)}, u32[]{:S(2)}, u32[]{:S(2)}) async-start(bf16[32,384,128]{2,1,0:T(8,128)(2,1)} %pack_main.1), calls=%async_computation.1 | async-start | bytes 6291456 | tf_op jit(solution)/shard_map/all_to_all | solution.py:279
  36.0 31.3 %collective-permute-start = (bf16[128,1024]{1,0:T(8,128)(2,1)S(1)}, bf16[128,1024]{1,0:T(8,128)(2,1)S(1)}, u32[]{:S(2)}, u32[]{:S(2)}) collective-permute-start(bf16[128,1024]{1,0:T(8,128)(2,1)S(1)} %get-tuple-element.9), channel_id=1, source_target_pairs={{96,0},{0,32},{32,64},{64,96},{97,1},{1,33},{33,65},{65,97},{98,2}... | collective-permute-start | bytes 786440 | tf_op jit(solution)/shard_map/ppermute | solution.py:346
